TPU v7x, 32 devices: a whole 2x2x4 slice. The times are simulated.
32 devices in a mesh: gx: 4 (over y, core), gy: 2 (over x), gz: 4 (over z).
Axes of the slice: x: 2, y: 2, z: 4, core: 2. Of those that a mesh axis runs over, the one named last changes fastest.
Arguments:
- orbitals: float32 [8, 32, 16, 512], P(None, 'gx', 'gy', 'gz'), may hold values from -6 to 6
- potential: float32 [32, 16, 512], P('gx', 'gy', 'gz'), may hold values from -3 to 0
- proj_values: float32 [4, 65536], P(None, ('gx', 'gy', 'gz')), may hold values from -1 to 1
- point_cell: int32 [65536], P(('gx', 'gy', 'gz')), may hold values from 0 to 8191
- point_owner: int32 [65536], P(('gx', 'gy', 'gz')), may hold values from 0 to 31, as said below
- point_slot: int32 [65536], P(('gx', 'gy', 'gz')), may hold values from 0 to 4
- point_count: int32 [32], P(('gx', 'gy', 'gz')), may hold values from 1 to 2048, 40960 in all
- atom_energy: float32 [4, 160], replicated, may hold values from -2 to 2
Outputs:
- filtered: float32 [8, 32, 16, 512], P(None, 'gx', 'gy', 'gz')
Inputs may be any that keep to these rules, and one draw needn't show every extreme that they name: `point_owner`: the owner of point i's atom differs from domain i // 2048 by at most one index along each of gx, gy and gz, counted periodically. Only the first point_count[d] of domain d's 2048 point slots are live; some domain has all of them live.
All inputs are finite; a program needn't handle non-finite values. No bound on the sum of `point_count` on one device may be relied on, other than what follows from the above.
Results may differ from a plain program's by a relative error of at most 0.0001.
Values sent between devices are 32-bit elements; how exact they have to be, the bound alone decides.
A program may use at most 64 MiB of HBM per device.

v0:
```python
import jax
import jax.numpy as jnp
from jax import lax
from jax.sharding import PartitionSpec as P

DEGREE = 3
ATOM_DEV = 5


stencil_terms = (
    -5369.0 / 1800.0,
    12.0 / 7.0,
    -15.0 / 56.0,
    10.0 / 189.0,
    -1.0 / 112.0,
    2.0 / 1925.0,
    -1.0 / 16632.0,
)
lowest = -3.5
cutoff = 1.5
highest = 13.0


def with_halo(cells, sides, width):
    for axis, dim in sides:
        count = lax.axis_size(axis)
        head = lax.slice_in_dim(cells, 0, width, axis=dim)
        tail = lax.slice_in_dim(cells, cells.shape[dim] - width, cells.shape[dim], axis=dim)
        cells = jnp.concatenate(
            [
                lax.ppermute(tail, axis, [(i, (i + 1) % count) for i in range(count)]),
                cells,
                lax.ppermute(head, axis, [((i + 1) % count, i) for i in range(count)]),
            ],
            axis=dim,
        )
    return cells


def shifted(value, axis, steps):
    count = lax.axis_size(axis)
    pairs = [(source, (source + steps) % count) for source in range(count)]
    return lax.ppermute(value, axis, pairs)


def second_sum(padded, along_dim, length):

    def window(first_index):
        return lax.slice_in_dim(padded, first_index, first_index + length, axis=along_dim)

    summed = stencil_terms[0] * window(6)
    for offset in range(1, 7):
        summed = summed + stencil_terms[offset] * (window(6 + offset) + window(6 - offset))
    return summed


def laplace_part(grid_field):
    padded = with_halo(grid_field, (("gx", 1), ("gy", 2), ("gz", 3)), 6)
    padded_x = padded[:, :, 6:-6, 6:-6]
    padded_y = padded[:, 6:-6, :, 6:-6]
    padded_z = padded[:, 6:-6, 6:-6, :]
    laplace = second_sum(padded_x, 1, grid_field.shape[1])
    laplace = laplace + second_sum(padded_y, 2, grid_field.shape[2])
    return laplace + second_sum(padded_z, 3, grid_field.shape[3])


def wrapped_offset(owner_coord, own_coord, axis_count):
    remain = (owner_coord - own_coord) % axis_count
    return jnp.where(remain == 0, 0, jnp.where(remain == 1, 1, -1)).astype(jnp.int32)


def body(
    orbitals, potential, proj_values, point_cell, point_owner, point_slot, point_count, atom_energy
):
    orbital_count = orbitals.shape[0]
    cell_count = orbitals.shape[1] * orbitals.shape[2] * orbitals.shape[3]
    projector_count = proj_values.shape[0]
    point_total = proj_values.shape[1]
    live_mask = (jnp.arange(point_total, dtype=jnp.int32) < point_count[0]).astype(jnp.float32)
    masked = proj_values * live_mask[None, :]
    masked_rows = masked.T
    size_x = lax.axis_size("gx")
    size_y = lax.axis_size("gy")
    size_z = lax.axis_size("gz")
    index_x = lax.axis_index("gx")
    index_y = lax.axis_index("gy")
    index_z = lax.axis_index("gz")
    owner_x = point_owner // (size_y * size_z)
    owner_y = point_owner // size_z % size_y
    owner_z = point_owner % size_z
    neighbour_code = (wrapped_offset(owner_x, index_x, size_x) + 1) * 9
    neighbour_code = neighbour_code + (wrapped_offset(owner_y, index_y, size_y) + 1) * 3
    neighbour_code = neighbour_code + wrapped_offset(owner_z, index_z, size_z) + 1
    neighbour_seg = neighbour_code * ATOM_DEV + point_slot
    domain = (index_x * size_y + index_y) * size_z + index_z
    own_energy = lax.dynamic_slice_in_dim(atom_energy, domain * ATOM_DEV, ATOM_DEV, 1).T

    def nonlocal_part(grid_field):
        flattened = grid_field.reshape(orbital_count, cell_count)
        sampled = flattened[:, point_cell]
        contributions = (
            (masked[:, None, :] * sampled[None, :, :])
            .reshape(projector_count * orbital_count, point_total)
            .T
        )
        partials = jax.ops.segment_sum(
            contributions, neighbour_seg, num_segments=27 * ATOM_DEV
        ).reshape(3, 3, 3, -1)
        plane_sum = partials[1]
        for offset, source in ((1, 2), (-1, 0)):
            plane_sum = plane_sum + shifted(partials[source], "gx", offset)
        line_sum = plane_sum[1]
        for offset, source in ((1, 2), (-1, 0)):
            line_sum = line_sum + shifted(plane_sum[source], "gy", offset)
        owned = line_sum[1]
        for offset, source in ((1, 2), (-1, 0)):
            owned = owned + shifted(line_sum[source], "gz", offset)
        coefficients = (
            owned.reshape(ATOM_DEV, projector_count, orbital_count) * own_energy[:, :, None]
        )
        neighbourhood = with_halo(
            coefficients.reshape(1, 1, 1, -1), (("gx", 0), ("gy", 1), ("gz", 2)), 1
        )
        atom_rows = neighbourhood.reshape(27 * ATOM_DEV, projector_count, orbital_count)[
            neighbour_seg
        ]
        returned = jnp.sum(masked_rows[:, :, None] * atom_rows, axis=1)
        return jnp.zeros_like(flattened).at[:, point_cell].add(returned.T).reshape(grid_field.shape)

    def hamiltonian(grid_field):
        return (
            -0.5 * laplace_part(grid_field)
            + potential[None] * grid_field
            + nonlocal_part(grid_field)
        )

    half_width = (highest - cutoff) / 2.0
    middle = (highest + cutoff) / 2.0
    sigma_first = half_width / (lowest - middle)
    previous = orbitals
    current = sigma_first / half_width * (hamiltonian(orbitals) - middle * orbitals)
    sigma_now = sigma_first
    for degree_index in range(1, DEGREE):
        sigma_next = 1.0 / (2.0 / sigma_first - sigma_now)
        following = (
            2.0 * sigma_next / half_width * (hamiltonian(current) - middle * current)
            - sigma_now * sigma_next * previous
        )
        previous = current
        current = following
        sigma_now = sigma_next
    return current


def solution(mesh):
    return jax.shard_map(
        body,
        mesh=mesh,
        in_specs=(
            P(None, "gx", "gy", "gz"),
            P("gx", "gy", "gz"),
            P(None, ("gx", "gy", "gz")),
            P(("gx", "gy", "gz")),
            P(("gx", "gy", "gz")),
            P(("gx", "gy", "gz")),
            P(("gx", "gy", "gz")),
            P(),
        ),
        out_specs=P(None, "gx", "gy", "gz"),
        check_vma=False,
    )
```

profile of v0, /device:TPU:0, one launch (start us, length us, event | category | flops | bytes accessed | tf_op | source)
XLA Modules:
  0.0 416.9 jit_solution(7469007072214965757)
XLA Ops:
  3.7 7.7 %gather_fusion = f32[2048,8]{1,0:T(8,128)S(1)} fusion(f32[8,8192]{0,1:T(8,128)} %bitcast.72, s32[2048]{0:T(1024)S(1)} %get-tuple-element.65), kind=kCustom, calls=%fused_computation | custom fusion | bytes 139264 | tf_op jit(solution)/shard_map/gather | solution.py:100
  12.7 11.5 %scatter_custom_fusion = f32[135,32]{1,0:T(8,128)S(1)} fusion(s32[2048]{0:T(1024)S(1)} %get-tuple-element.8, f32[2048,32]{1,0:T(8,128)S(1)} %copy.46, f32[]{:T(128)} %constant.106.clone.1), kind=kCustom, calls=%fused_computation.347 | custom fusion | flops 65536 | bytes 17284 | tf_op jit(solution)/shard_map/scatter-add | solution.py:106
  40.0 4.1 collective-permute-done.10
  58.1 15.3 %gather_fusion.1 = f32[2048,4,8]{2,1,0:T(4,128)} fusion(f32[135,4,8]{2,1,0:T(4,128)S(1)} %reshape.97, s32[2048]{0:T(1024)S(1)} %get-tuple-element.7), kind=kCustom, calls=%fused_computation.1 | custom fusion | bytes 532480 | tf_op jit(solution)/shard_map/gather | solution.py:124
  73.3 5.1 %collective-permute-done.3 = f32[8,20,6,128]{3,0,2,1:T(8,128)} collective-permute-done((f32[8,20,6,128]{3,0,2,1:T(8,128)}, f32[8,20,6,128]{3,0,2,1:T(8,128)}, u32[]{:S(2)}, u32[]{:S(2)}) %collective-permute-start.3) | collective-permute-done | bytes 491552 | tf_op jit(solution)/shard_map/ppermute | solution.py:31
  92.7 13.3 %multiply_reduce_fusion.2 = f32[2048,8]{1,0:T(8,128)} fusion(f32[2048,4,8]{2,1,0:T(4,128)} %gather_fusion.1, f32[2048,4]{1,0:T(8,128)S(1)} %copy.43), kind=kLoop, calls=%fused_computation.14 | loop fusion | flops 114688 | bytes 360448 | tf_op jit(solution)/shard_map/reduce_sum | solution.py:127
  106.0 14.0 %scatter_custom_fusion.1 = f32[8,8192]{0,1:T(8,128)} fusion(s32[2048]{0:T(1024)S(1)} %get-tuple-element.64, f32[2048,8]{1,0:T(8,128)} %multiply_reduce_fusion.2, f32[]{:T(128)} %constant.106.clone.1), kind=kCustom, calls=%fused_computation.29 | custom fusion | flops 16384 | bytes 262656 | tf_op jit(solution)/shard_map/scatter-add | solution.py:128
  129.5 5.5 %broadcast_multiply_fusion = (f32[8,8,8,128]{3,0,2,1:T(8,128)S(1)}, f32[8,8,8,128]{3,0,2,1:T(8,128)}) fusion(f32[8,8,8,128]{3,0,2,1:T(8,128)S(1)} %copy.48, f32[8,8,128]{2,1,0:T(8,128)S(1)} %copy-done.10, f32[8,20,6,128]{3,0,2,1:T(8,128)} %copy-done.9, f32[8,20,8,128]{3,0,2,1:T(8,128)S(1)} %get-tuple-element.35, ...), kind=kLoop, calls=%fused_computation.339 | loop fusion | flops 7340032 | bytes 6019072 | tf_op jit(solution)/shard_map/mul | solution.py:141
  137.6 9.8 %gather_fusion.2 = f32[2048,8]{1,0:T(8,128)} fusion(f32[8,8192]{0,1:T(8,128)} %bitcast.74, s32[2048]{0:T(1024)S(1)} %get-tuple-element.65), kind=kCustom, calls=%fused_computation.2 | custom fusion | bytes 139264 | tf_op jit(solution)/shard_map/gather | solution.py:100
  150.3 11.8 %scatter_custom_fusion.2 = f32[135,32]{1,0:T(8,128)S(1)} fusion(s32[2048]{0:T(1024)} %copy-done.16, f32[2048,32]{1,0:T(8,128)} %copy.56, f32[]{:T(128)} %constant.106.clone.1), kind=kCustom, calls=%fused_computation.345 | custom fusion | flops 65536 | bytes 17792 | tf_op jit(solution)/shard_map/scatter-add | solution.py:106
  189.4 15.3 %gather_fusion.3 = f32[2048,4,8]{2,1,0:T(4,128)} fusion(f32[135,4,8]{2,1,0:T(4,128)S(1)} %reshape.100, s32[2048]{0:T(1024)S(1)} %get-tuple-element.7), kind=kCustom, calls=%fused_computation.3 | custom fusion | bytes 532480 | tf_op jit(solution)/shard_map/gather | solution.py:124
  207.8 13.3 %multiply_reduce_fusion.1 = f32[2048,8]{1,0:T(8,128)} fusion(f32[2048,4,8]{2,1,0:T(4,128)} %gather_fusion.3, f32[2048,4]{1,0:T(8,128)S(1)} %copy.43), kind=kLoop, calls=%fused_computation.13 | loop fusion | flops 114688 | bytes 360448 | tf_op jit(solution)/shard_map/reduce_sum | solution.py:127
  221.1 14.0 %scatter_custom_fusion.3 = f32[8,8192]{0,1:T(8,128)} fusion(s32[2048]{0:T(1024)S(1)} %get-tuple-element.64, f32[2048,8]{1,0:T(8,128)} %multiply_reduce_fusion.1, f32[]{:T(128)} %constant.106.clone.1), kind=kCustom, calls=%fused_computation.27 | custom fusion | flops 16384 | bytes 262656 | tf_op jit(solution)/shard_map/scatter-add | solution.py:128
  247.9 4.1 collective-permute-start.22
  253.5 7.1 %collective-permute-done.23 = f32[8,20,20,6]{2,0,3,1:T(8,128)} collective-permute-done((f32[8,20,20,6]{2,0,3,1:T(8,128)}, f32[8,20,20,6]{2,0,3,1:T(8,128)}, u32[]{:S(2)}, u32[]{:S(2)}) %collective-permute-start.23) | collective-permute-done | bytes 76832 | tf_op jit(solution)/shard_map/ppermute | solution.py:31
  270.4 6.0 %fusion.52 = f32[8,8,8,128]{3,0,2,1:T(8,128)S(1)} fusion(f32[8,8,8,128]{3,0,2,1:T(8,128)} %copy.57, f32[8,8,8,128]{3,0,2,1:T(8,128)S(1)} %get-tuple-element.5, f32[8,6,8,128]{3,0,2,1:T(8,128)S(1)} %collective-permute-done.19, f32[8,6,8,128]{3,0,2,1:T(8,128)S(1)} %copy-done.8, f32[8,20,20,6]{3,0,2,1:T(8,128)} %copy.53, ...), kind=kLoop, calls=%fused_computation.136 | loop fusion | flops 9043968 | bytes 6019072 | tf_op jit(solution)/shard_map/sub | solution.py:146
  279.1 7.6 %gather_fusion.4 = f32[2048,8]{1,0:T(8,128)S(1)} fusion(f32[8,8192]{0,1:T(8,128)} %bitcast.73, s32[2048]{0:T(1024)S(1)} %get-tuple-element.65), kind=kCustom, calls=%fused_computation.4 | custom fusion | bytes 139264 | tf_op jit(solution)/shard_map/gather | solution.py:100
  287.4 11.6 %scatter_custom_fusion.4 = f32[135,32]{1,0:T(8,128)S(1)} fusion(s32[2048]{0:T(1024)} %copy-done.16, f32[2048,32]{1,0:T(8,128)S(1)} %copy.65, f32[]{:T(128)} %constant.106.clone.1), kind=kCustom, calls=%fused_computation.343 | custom fusion | flops 65536 | bytes 17792 | tf_op jit(solution)/shard_map/scatter-add | solution.py:106
  326.3 15.3 %gather_fusion.5 = f32[2048,4,8]{2,1,0:T(4,128)} fusion(f32[135,4,8]{2,1,0:T(4,128)S(1)} %reshape.103, s32[2048]{0:T(1024)S(1)} %get-tuple-element.7), kind=kCustom, calls=%fused_computation.5 | custom fusion | bytes 532480 | tf_op jit(solution)/shard_map/gather | solution.py:124
  344.7 13.3 %multiply_reduce_fusion = f32[2048,8]{1,0:T(8,128)} fusion(f32[2048,4,8]{2,1,0:T(4,128)} %gather_fusion.5, f32[2048,4]{1,0:T(8,128)S(1)} %copy.43), kind=kLoop, calls=%fused_computation.12 | loop fusion | flops 114688 | bytes 360448 | tf_op jit(solution)/shard_map/reduce_sum | solution.py:127
  358.1 14.0 %scatter_custom_fusion.5 = f32[8,8192]{0,1:T(8,128)} fusion(s32[2048]{0:T(1024)S(1)} %get-tuple-element.64, f32[2048,8]{1,0:T(8,128)} %multiply_reduce_fusion, f32[]{:T(128)} %constant.106.clone.1), kind=kCustom, calls=%fused_computation.25 | custom fusion | flops 16384 | bytes 262656 | tf_op jit(solution)/shard_map/scatter-add | solution.py:128
  390.9 7.8 %collective-permute-done.41 = f32[8,20,20,6]{2,0,3,1:T(8,128)} collective-permute-done((f32[8,20,20,6]{2,0,3,1:T(8,128)}, f32[8,20,20,6]{2,0,3,1:T(8,128)}, u32[]{:S(2)}, u32[]{:S(2)}) %collective-permute-start.41) | collective-permute-done | bytes 76832 | tf_op jit(solution)/shard_map/ppermute | solution.py:31
  400.8 5.3 %collective-permute-done.40 = f32[8,20,20,6]{2,0,3,1:T(8,128)} collective-permute-done((f32[8,20,20,6]{2,0,3,1:T(8,128)}, f32[8,20,20,6]{2,0,3,1:T(8,128)}, u32[]{:S(2)}, u32[]{:S(2)}) %collective-permute-start.40) | collective-permute-done | bytes 76832 | tf_op jit(solution)/shard_map/ppermute | solution.py:33
  409.4 6.5 %fusion.18 = f32[8,8,8,128]{3,0,2,1:T(8,128)S(1)} fusion(f32[8,8,8,128]{3,0,2,1:T(8,128)} %copy.66, f32[8,8,8,128]{3,0,2,1:T(8,128)S(1)} %fusion.52, f32[8,6,8,128]{3,0,2,1:T(8,128)S(1)} %collective-permute-done.37, f32[8,6,8,128]{3,0,2,1:T(8,128)} %copy-done.6, f32[8,20,20,6]{3,0,2,1:T(8,128)S(1)} %copy.62, f32[8,20,6,128]{3,0,2,1:T(8,128)} %copy-done.4, ...), kind=kLoop, calls=%fused_computation.102 | loop fusion | flops 9043968 | bytes 5756928 | tf_op jit(solution)/shard_map/sub | solution.py:146
  (234 shorter events, 176.1 us)
Async XLA Ops:
  38.7 5.4 %collective-permute-start.10 = (f32[160]{0:T(256)S(1)}, f32[160]{0:T(256)S(1)}, u32[]{:S(2)}, u32[]{:S(2)}) collective-permute-start(f32[160]{0:T(256)S(1)} %bitcast.96), channel_id=1, source_target_pairs={{0,1},{1,2},{2,3},{3,0},{4,5},{5,6},{6,7},{7,4},{8,9},{9,10},{10,1... | collective-permute-start | bytes 1928 | tf_op jit(solution)/shard_map/ppermute | solution.py:43
  44.7 8.7 %collective-permute-start.1 = (f32[8,6,8,128]{3,0,2,1:T(8,128)S(1)}, f32[8,6,8,128]{3,0,2,1:T(8,128)S(1)}, u32[]{:S(2)}, u32[]{:S(2)}) collective-permute-start(f32[8,6,8,128]{3,0,2,1:T(8,128)S(1)} %copy.73), channel_id=1, source_target_pairs={{0,8},{8,16},{16,24},{24,0},{1,9},{9,17},{17,25},{25,1},{2,10},{10... | collective-permute-start | bytes 589832 | tf_op jit(solution)/shard_map/ppermute | solution.py:31
  51.3 6.5 %collective-permute-start.17 = (f32[3,3,1,160]{3,2,1,0:T(1,128)S(1)}, f32[3,3,1,160]{3,2,1,0:T(1,128)S(1)}, u32[]{:S(2)}, u32[]{:S(2)}) collective-permute-start(f32[3,3,1,160]{3,2,1,0:T(1,128)S(1)} %pad_maximum_fusion.42), channel_id=1, source_target_pairs={{1,0},{2,1},{3,2},{0,3},{5,4},{6,5},{7,6},{4,7},{9,8},{10,9},{11,1... | collective-permute-start | bytes 17288 | tf_op jit(solution)/shard_map/ppermute | solution.py:33
  51.4 6.4 %collective-permute-start.16 = (f32[3,3,1,160]{3,2,1,0:T(1,128)S(1)}, f32[3,3,1,160]{3,2,1,0:T(1,128)S(1)}, u32[]{:S(2)}, u32[]{:S(2)}) collective-permute-start(f32[3,3,1,160]{3,2,1,0:T(1,128)S(1)} %pad_maximum_fusion.42), channel_id=1, source_target_pairs={{0,1},{1,2},{2,3},{3,0},{4,5},{5,6},{6,7},{7,4},{8,9},{9,10},{10,1... | collective-permute-start | bytes 17288 | tf_op jit(solution)/shard_map/ppermute | solution.py:31
  55.4 17.9 %collective-permute-start.2 = (f32[8,20,6,128]{3,0,2,1:T(8,128)}, f32[8,20,6,128]{3,0,2,1:T(8,128)S(1)}, u32[]{:S(2)}, u32[]{:S(2)}) collective-permute-start(f32[8,20,6,128]{3,0,2,1:T(8,128)} %get-tuple-element.24), channel_id=1, source_target_pairs={{4,0},{0,4},{5,1},{1,5},{6,2},{2,6},{7,3},{3,7},{12,8},{8,12},{13,... | collective-permute-start | bytes 1474568 | tf_op jit(solution)/shard_map/ppermute | solution.py:33
  56.9 21.6 %collective-permute-start.3 = (f32[8,20,6,128]{3,0,2,1:T(8,128)}, f32[8,20,6,128]{3,0,2,1:T(8,128)}, u32[]{:S(2)}, u32[]{:S(2)}) collective-permute-start(f32[8,20,6,128]{3,0,2,1:T(8,128)} %get-tuple-element.23), channel_id=1, source_target_pairs={{0,4},{4,0},{1,5},{5,1},{2,6},{6,2},{3,7},{7,3},{8,12},{12,8},{9,1... | collective-permute-start | bytes 1474568 | tf_op jit(solution)/shard_map/ppermute | solution.py:31
  85.4 37.5 %collective-permute-start.5 = (f32[8,20,20,6]{2,0,3,1:T(8,128)}, f32[8,20,20,6]{2,0,3,1:T(8,128)}, u32[]{:S(2)}, u32[]{:S(2)}) collective-permute-start(f32[8,20,20,6]{2,0,3,1:T(8,128)} %copy.40), channel_id=1, source_target_pairs={{0,1},{1,2},{2,3},{3,0},{4,5},{5,6},{6,7},{7,4},{8,9},{9,10},{10,1... | collective-permute-start | bytes 230408 | tf_op jit(solution)/shard_map/ppermute | solution.py:31
  88.7 37.5 %collective-permute-start.4 = (f32[8,20,20,6]{2,0,3,1:T(8,128)}, f32[8,20,20,6]{2,0,3,1:T(8,128)}, u32[]{:S(2)}, u32[]{:S(2)}) collective-permute-start(f32[8,20,20,6]{2,0,3,1:T(8,128)} %copy.38), channel_id=1, source_target_pairs={{1,0},{2,1},{3,2},{0,3},{5,4},{6,5},{7,6},{4,7},{9,8},{10,9},{11,1... | collective-permute-start | bytes 230408 | tf_op jit(solution)/shard_map/ppermute | solution.py:33
  169.7 5.4 %collective-permute-start.28 = (f32[160]{0:T(256)S(1)}, f32[160]{0:T(256)S(1)}, u32[]{:S(2)}, u32[]{:S(2)}) collective-permute-start(f32[160]{0:T(256)S(1)} %bitcast.98), channel_id=1, source_target_pairs={{0,1},{1,2},{2,3},{3,0},{4,5},{5,6},{6,7},{7,4},{8,9},{9,10},{10,1... | collective-permute-start | bytes 1928 | tf_op jit(solution)/shard_map/ppermute | solution.py:43
  180.3 24.4 %collective-permute-start.19 = (f32[8,6,8,128]{3,0,2,1:T(8,128)S(1)}, f32[8,6,8,128]{3,0,2,1:T(8,128)S(1)}, u32[]{:S(2)}, u32[]{:S(2)}) collective-permute-start(f32[8,6,8,128]{3,0,2,1:T(8,128)S(1)} %get-tuple-element.28), channel_id=1, source_target_pairs={{0,8},{8,16},{16,24},{24,0},{1,9},{9,17},{17,25},{25,1},{2,10},{10... | collective-permute-start | bytes 589832 | tf_op jit(solution)/shard_map/ppermute | solution.py:31
  180.3 24.3 %collective-permute-start.18 = (f32[8,6,8,128]{3,0,2,1:T(8,128)S(1)}, f32[8,6,8,128]{3,0,2,1:T(8,128)S(1)}, u32[]{:S(2)}, u32[]{:S(2)}) collective-permute-start(f32[8,6,8,128]{3,0,2,1:T(8,128)S(1)} %get-tuple-element.27), channel_id=1, source_target_pairs={{8,0},{16,8},{24,16},{0,24},{9,1},{17,9},{25,17},{1,25},{10,2},{18... | collective-permute-start | bytes 589832 | tf_op jit(solution)/shard_map/ppermute | solution.py:33
  183.4 5.8 %collective-permute-start.34 = (f32[3,3,1,160]{3,2,1,0:T(1,128)S(1)}, f32[3,3,1,160]{3,2,1,0:T(1,128)S(1)}, u32[]{:S(2)}, u32[]{:S(2)}) collective-permute-start(f32[3,3,1,160]{3,2,1,0:T(1,128)S(1)} %pad_maximum_fusion.43), channel_id=1, source_target_pairs={{0,1},{1,2},{2,3},{3,0},{4,5},{5,6},{6,7},{7,4},{8,9},{9,10},{10,1... | collective-permute-start | bytes 17288 | tf_op jit(solution)/shard_map/ppermute | solution.py:31
  205.7 32.8 %collective-permute-start.20 = (f32[8,20,6,128]{3,0,2,1:T(8,128)}, f32[8,20,6,128]{3,0,2,1:T(8,128)S(1)}, u32[]{:S(2)}, u32[]{:S(2)}) collective-permute-start(f32[8,20,6,128]{3,0,2,1:T(8,128)} %get-tuple-element.22), channel_id=1, source_target_pairs={{4,0},{0,4},{5,1},{1,5},{6,2},{2,6},{7,3},{3,7},{12,8},{8,12},{13,... | collective-permute-start | bytes 1474568 | tf_op jit(solution)/shard_map/ppermute | solution.py:33
  206.3 32.3 %collective-permute-start.21 = (f32[8,20,6,128]{3,0,2,1:T(8,128)}, f32[8,20,6,128]{3,0,2,1:T(8,128)S(1)}, u32[]{:S(2)}, u32[]{:S(2)}) collective-permute-start(f32[8,20,6,128]{3,0,2,1:T(8,128)} %get-tuple-element.21), channel_id=1, source_target_pairs={{0,4},{4,0},{1,5},{5,1},{2,6},{6,2},{3,7},{7,3},{8,12},{12,8},{9,1... | collective-permute-start | bytes 1474568 | tf_op jit(solution)/shard_map/ppermute | solution.py:31
  244.4 16.3 %collective-permute-start.23 = (f32[8,20,20,6]{2,0,3,1:T(8,128)}, f32[8,20,20,6]{2,0,3,1:T(8,128)}, u32[]{:S(2)}, u32[]{:S(2)}) collective-permute-start(f32[8,20,20,6]{2,0,3,1:T(8,128)} %copy.52), channel_id=1, source_target_pairs={{0,1},{1,2},{2,3},{3,0},{4,5},{5,6},{6,7},{7,4},{8,9},{9,10},{10,1... | collective-permute-start | bytes 230408 | tf_op jit(solution)/shard_map/ppermute | solution.py:31
  247.9 19.3 %collective-permute-start.22 = (f32[8,20,20,6]{2,0,3,1:T(8,128)}, f32[8,20,20,6]{2,0,3,1:T(8,128)}, u32[]{:S(2)}, u32[]{:S(2)}) collective-permute-start(f32[8,20,20,6]{2,0,3,1:T(8,128)} %copy.50), channel_id=1, source_target_pairs={{1,0},{2,1},{3,2},{0,3},{5,4},{6,5},{7,6},{4,7},{9,8},{10,9},{11,1... | collective-permute-start | bytes 230408 | tf_op jit(solution)/shard_map/ppermute | solution.py:33
  307.7 5.4 %collective-permute-start.46 = (f32[160]{0:T(256)S(1)}, f32[160]{0:T(256)S(1)}, u32[]{:S(2)}, u32[]{:S(2)}) collective-permute-start(f32[160]{0:T(256)S(1)} %bitcast.99), channel_id=1, source_target_pairs={{0,1},{1,2},{2,3},{3,0},{4,5},{5,6},{6,7},{7,4},{8,9},{9,10},{10,1... | collective-permute-start | bytes 1928 | tf_op jit(solution)/shard_map/ppermute | solution.py:43
  318.3 23.3 %collective-permute-start.37 = (f32[8,6,8,128]{3,0,2,1:T(8,128)S(1)}, f32[8,6,8,128]{3,0,2,1:T(8,128)S(1)}, u32[]{:S(2)}, u32[]{:S(2)}) collective-permute-start(f32[8,6,8,128]{3,0,2,1:T(8,128)S(1)} %get-tuple-element.26), channel_id=1, source_target_pairs={{0,8},{8,16},{16,24},{24,0},{1,9},{9,17},{17,25},{25,1},{2,10},{10... | collective-permute-start | bytes 589832 | tf_op jit(solution)/shard_map/ppermute | solution.py:31
  318.3 23.3 %collective-permute-start.36 = (f32[8,6,8,128]{3,0,2,1:T(8,128)S(1)}, f32[8,6,8,128]{3,0,2,1:T(8,128)S(1)}, u32[]{:S(2)}, u32[]{:S(2)}) collective-permute-start(f32[8,6,8,128]{3,0,2,1:T(8,128)S(1)} %get-tuple-element.25), channel_id=1, source_target_pairs={{8,0},{16,8},{24,16},{0,24},{9,1},{17,9},{25,17},{1,25},{10,2},{18... | collective-permute-start | bytes 589832 | tf_op jit(solution)/shard_map/ppermute | solution.py:33
  320.5 5.6 %collective-permute-start.52 = (f32[3,3,1,160]{3,2,1,0:T(1,128)S(1)}, f32[3,3,1,160]{3,2,1,0:T(1,128)S(1)}, u32[]{:S(2)}, u32[]{:S(2)}) collective-permute-start(f32[3,3,1,160]{3,2,1,0:T(1,128)S(1)} %pad_maximum_fusion.44), channel_id=1, source_target_pairs={{0,1},{1,2},{2,3},{3,0},{4,5},{5,6},{6,7},{7,4},{8,9},{9,10},{10,1... | collective-permute-start | bytes 17288 | tf_op jit(solution)/shard_map/ppermute | solution.py:31
  342.7 32.9 %collective-permute-start.38 = (f32[8,20,6,128]{3,0,2,1:T(8,128)}, f32[8,20,6,128]{3,0,2,1:T(8,128)S(1)}, u32[]{:S(2)}, u32[]{:S(2)}) collective-permute-start(f32[8,20,6,128]{3,0,2,1:T(8,128)} %get-tuple-element.18), channel_id=1, source_target_pairs={{4,0},{0,4},{5,1},{1,5},{6,2},{2,6},{7,3},{3,7},{12,8},{8,12},{13,... | collective-permute-start | bytes 1474568 | tf_op jit(solution)/shard_map/ppermute | solution.py:33
  344.2 31.3 %collective-permute-start.39 = (f32[8,20,6,128]{3,0,2,1:T(8,128)}, f32[8,20,6,128]{3,0,2,1:T(8,128)S(1)}, u32[]{:S(2)}, u32[]{:S(2)}) collective-permute-start(f32[8,20,6,128]{3,0,2,1:T(8,128)} %get-tuple-element.17), channel_id=1, source_target_pairs={{0,4},{4,0},{1,5},{5,1},{2,6},{6,2},{3,7},{7,3},{8,12},{12,8},{9,1... | collective-permute-start | bytes 1474568 | tf_op jit(solution)/shard_map/ppermute | solution.py:31
  382.4 16.3 %collective-permute-start.41 = (f32[8,20,20,6]{2,0,3,1:T(8,128)}, f32[8,20,20,6]{2,0,3,1:T(8,128)}, u32[]{:S(2)}, u32[]{:S(2)}) collective-permute-start(f32[8,20,20,6]{2,0,3,1:T(8,128)} %copy.61), channel_id=1, source_target_pairs={{0,1},{1,2},{2,3},{3,0},{4,5},{5,6},{6,7},{7,4},{8,9},{9,10},{10,1... | collective-permute-start | bytes 230408 | tf_op jit(solution)/shard_map/ppermute | solution.py:31
  384.5 21.6 %collective-permute-start.40 = (f32[8,20,20,6]{2,0,3,1:T(8,128)}, f32[8,20,20,6]{2,0,3,1:T(8,128)}, u32[]{:S(2)}, u32[]{:S(2)}) collective-permute-start(f32[8,20,20,6]{2,0,3,1:T(8,128)} %copy.59), channel_id=1, source_target_pairs={{1,0},{2,1},{3,2},{0,3},{5,4},{6,5},{7,6},{4,7},{9,8},{10,9},{11,1... | collective-permute-start | bytes 230408 | tf_op jit(solution)/shard_map/ppermute | solution.py:33
  (47 other events, 335.2 us)
where the time goes:
time: 424 us; the launch traced here: 417 us
  local copies, waits for them, and re-layouts  146 us (34%)
  other arithmetic  142 us (33%)
  waiting for transfers between devices  74 us (17%)
  starting transfers between devices  54.1 us (13%)
    gather x3, local copies, waits for them, and re-layouts, nonlocal_part(): neighbourhood.reshape(27 * ATOM_DEV, projector_count, orbital_count)  45.8 us
    scatter-add x3, other arithmetic, nonlocal_part(): jnp.zeros_like(flattened).at[:, point_cell].add(returned.T)  42.1 us
    reduce_sum x3, other arithmetic, nonlocal_part(): returned = jnp.sum(masked_rows[:, :, None] * atom_rows, axis=1)  40 us
    scatter-add x3, other arithmetic, nonlocal_part(): jax.ops.segment_sum(contributions, neighbour_seg, num_segments=27 * ATOM_...  34.8 us
    ppermute x18, waiting for transfers between devices, with_halo(): lax.ppermute(tail, axis, [(i, (i + 1) % count) for i in range(count)])  31.5 us
    ppermute x18, waiting for transfers between devices, shifted(): return lax.ppermute(value, axis, pairs)  28.4 us
    gather x6, local copies, waits for them, and re-layouts, nonlocal_part(): sampled = flattened[:, point_cell]  27.2 us
    ppermute x18, starting transfers between devices, with_halo(): lax.ppermute(head, axis, [((i + 1) % count, i) for i in range(count)])  22 us
  transfers between devices with their start and end apart: 54, of which 37 were waited for; matrix products, arithmetic and copies ran while one was open for 39% of the time, Pallas kernels for 0%

commit v1 on v0

v1 whole, which is shorter than its diff:
```python
import functools

import jax
import jax.numpy as jnp
from jax import lax
from jax.experimental import pallas as pl
from jax.experimental.pallas import tpu as pltpu
from jax.sharding import PartitionSpec as P

DEGREE = 3
ATOM_DEV = 5
WIDTH = 6
CHUNK = 512
MESH = pl.DeviceIdType.MESH
F32 = jnp.float32
BF16 = jnp.bfloat16
EXACT = lax.Precision.HIGHEST

stencil_terms = (
    -5369.0 / 1800.0,
    12.0 / 7.0,
    -15.0 / 56.0,
    10.0 / 189.0,
    -1.0 / 112.0,
    2.0 / 1925.0,
    -1.0 / 16632.0,
)
lowest = -3.5
cutoff = 1.5
highest = 13.0


def step_factors():
    half = (highest - cutoff) / 2.0
    middle = (highest + cutoff) / 2.0
    first = half / (lowest - middle)
    factors = [(first / half, 0.0)]
    sigma = first
    for _ in range(1, DEGREE):
        following = 1.0 / (2.0 / first - sigma)
        factors.append((2.0 * following / half, -sigma * following))
        sigma = following
    return middle, factors


def split_two(value):
    high = value.astype(BF16)
    low = (value - high.astype(F32)).astype(BF16)
    return high, low


def by_distance(distance):
    result = jnp.zeros(distance.shape, F32)
    for offset in range(WIDTH + 1):
        weight = 0.0 if offset == 0 else -0.5 * stencil_terms[offset]
        result = jnp.where(jnp.abs(distance) == offset, weight, result)
    return result


def kernel(
    sizes,
    orb_ref, pot_ref, val_ref, cell_ref, owner_ref, slot_ref, count_ref, energy_ref,
    out_ref,
    field, x_low, x_high, y_in, z_out, z_in, part_out, part_in, coef_out, coef_in,
    lane_hot, row_hot, seg_hot, masked, send_sem, recv_sem,
):
    size_x, size_y, size_z = sizes
    norb, cx, cy, cz = orb_ref.shape
    nproj, points = val_ref.shape
    rows = cx * cy
    spans = [min(3, size) for size in sizes]
    codes = [(a, b, c) for a in range(spans[0]) for b in range(spans[1]) for c in range(spans[2])]
    blocks = len(codes)
    seg_rows = seg_hot.shape[0]
    here = [lax.axis_index(name) for name in ("gx", "gy", "gz")]
    names = ("gx", "gy", "gz")

    def moved(axis, code):
        step = (0, 1, sizes[axis] - 1)[code]
        return lax.rem(here[axis] + step, sizes[axis])

    def device(code):
        return {name: moved(axis, code[axis]) for axis, name in enumerate(names)}

    def opposite(code):
        back = [0 if c == 0 else (1 if sizes[a] == 2 else 3 - c) for a, c in enumerate(code)]
        return codes.index(tuple(back))

    barrier = pltpu.get_barrier_semaphore()
    for code in codes[1:]:
        pl.semaphore_signal(barrier, inc=1, device_id=device(code), device_id_type=MESH)

    cells = cell_ref[...]
    lanes_of = cells % cz
    rows_of = cells // cz
    at_lane = (lax.broadcasted_iota(jnp.int32, (cz, points), 0) == lanes_of).astype(F32).astype(BF16)
    lane_hot[0:cz, :] = at_lane
    lane_hot[cz:2 * cz, :] = at_lane
    row_hot[...] = (lax.broadcasted_iota(jnp.int32, (rows, points), 0) == rows_of).astype(F32)
    owner = owner_ref[...]
    coords = (owner // (size_y * size_z), owner // size_z % size_y, owner % size_z)
    block = jnp.zeros_like(owner)
    for axis in range(3):
        remain = (coords[axis] - here[axis] + sizes[axis]) % sizes[axis]
        block = block * spans[axis] + jnp.minimum(remain, 2)
    segment = block * 8 + slot_ref[...]
    seg_hot[...] = (
        lax.broadcasted_iota(jnp.int32, (seg_rows, points), 0) == segment
    ).astype(F32).astype(BF16)
    live = lax.broadcasted_iota(jnp.int32, (nproj, points), 1) < count_ref[0]
    masked[...] = jnp.where(live, val_ref[...], 0.0)

    atoms = energy_ref.shape[1]
    domain = (here[0] * size_y + here[1]) * size_z + here[2]
    slots = lax.broadcasted_iota(jnp.int32, (8, atoms), 0)
    mine = (lax.broadcasted_iota(jnp.int32, (8, atoms), 1) == domain * ATOM_DEV + slots) & (
        slots < ATOM_DEV
    )
    lane_group = lax.broadcasted_iota(jnp.int32, (8, 128), 1) // norb
    energies = jnp.zeros((8, 128), F32)
    for j in range(nproj):
        own = jnp.sum(jnp.where(mine, energy_ref[j:j + 1, :], 0.0), axis=1, keepdims=True)
        energies = jnp.where(lane_group == j, own, energies)

    first = lax.broadcasted_iota(jnp.int32, (cz, cz), 0)
    second = lax.broadcasted_iota(jnp.int32, (cz, cz), 1)
    band = by_distance(first - second)
    place = lax.broadcasted_iota(jnp.int32, (16, cz), 0)
    lane = lax.broadcasted_iota(jnp.int32, (16, cz), 1)
    edge_band = by_distance(jnp.where(place < 8, place - 8, place - 8 + cz) - lane)
    edge_pick = (lane == jnp.where(place < 8, place, place - 16 + cz)).astype(F32)

    pl.semaphore_wait(barrier, blocks - 1)

    middle, factors = step_factors()
    started = []

    def send(step, index, source, target, device_id):
        copy = pltpu.make_async_remote_copy(
            src_ref=source,
            dst_ref=target,
            send_sem=send_sem.at[step, index],
            recv_sem=recv_sem.at[step, index],
            device_id=device_id,
            device_id_type=MESH,
        )
        copy.start()
        started.append(copy)
        return copy

    for step in range(DEGREE):
        source = orb_ref if step == 0 else field.at[step - 1]
        up = [{names[axis]: moved(axis, 1)} for axis in range(3)]
        down = [{names[axis]: lax.rem(here[axis] + sizes[axis] - 1, sizes[axis])} for axis in range(3)]
        y_copies = [send(step, 2, source, y_in.at[step, 0], up[1])]
        if size_y > 2:
            y_copies.append(send(step, 3, source, y_in.at[step, 1], down[1]))
        x_copies = [
            send(step, 0, source.at[:, pl.ds(cx - WIDTH, WIDTH)], x_low.at[step], up[0]),
            send(step, 1, source.at[:, pl.ds(0, WIDTH)], x_high.at[step], down[0]),
        ]
        flat = source[...].reshape(norb * rows, cz)
        z_out[step] = lax.dot_general(
            edge_pick, flat, (((1,), (1,)), ((), ())), precision=EXACT, preferred_element_type=F32
        ).reshape(2, 8, norb * rows)
        z_copies = [
            send(step, 4, z_out.at[step, 1], z_in.at[step, 0], up[2]),
            send(step, 5, z_out.at[step, 0], z_in.at[step, 1], down[2]),
        ]

        high, low = split_two(flat)
        both = jnp.concatenate([high, low], axis=1)
        weighted = []
        for begin in range(0, points, CHUNK):
            span = slice(begin, begin + CHUNK)
            spread = jnp.dot(both, lane_hot[:, span], preferred_element_type=F32)
            sampled = jnp.sum(
                spread.reshape(norb, rows, CHUNK) * row_hot[:, span][None], axis=1
            )
            weighted.append(
                jnp.concatenate([sampled * masked[j:j + 1, span] for j in range(nproj)], axis=0)
            )
        weighted = jnp.concatenate(weighted, axis=1)
        high, low = split_two(weighted)
        filler = jnp.zeros((128 - 2 * nproj * norb, points), BF16)
        partial = lax.dot_general(
            seg_hot[...],
            jnp.concatenate([high, low, filler], axis=0),
            (((1,), (1,)), ((), ())),
            preferred_element_type=F32,
        )
        partial = partial + pltpu.roll(partial, 128 - nproj * norb, 1)
        part_out[step] = partial[0:blocks * 8].reshape(blocks, 8, 128)
        part_copies = [
            send(step, 6 + n, part_out.at[step, n], part_in.at[step, n], device(codes[n]))
            for n in range(1, blocks)
        ]

        local = (pot_ref[...][None] + (-1.5 * stencil_terms[0] - middle)) * source[...]
        local = local + jnp.dot(
            flat, band, precision=EXACT, preferred_element_type=F32
        ).reshape(norb, cx, cy, cz)
        for copy in z_copies:
            copy.wait_recv()
        edges = z_in[step].reshape(16, norb * rows)
        local = local + jnp.dot(
            edges.T, edge_band, precision=EXACT, preferred_element_type=F32
        ).reshape(norb, cx, cy, cz)

        owned = partial[0:8]
        for n, copy in enumerate(part_copies, 1):
            copy.wait_recv()
            owned = owned + part_in[step, n]
        coefficients = owned * energies
        coef_out[step] = coefficients
        coef_copies = [
            send(
                step, 6 + blocks + n, coef_out.at[step], coef_in.at[step, opposite(codes[n])],
                device(codes[n]),
            )
            for n in range(1, blocks)
        ]

        for copy in x_copies:
            copy.wait_recv()
        along = jnp.concatenate([x_low[step], source[...], x_high[step]], axis=1)
        for offset in range(1, WIDTH + 1):
            local = local + (-0.5 * stencil_terms[offset]) * (
                along[:, WIDTH + offset:WIDTH + offset + cx]
                + along[:, WIDTH - offset:WIDTH - offset + cx]
            )
        for copy in y_copies:
            copy.wait_recv()
        below = y_in[step, 0]
        above = below if size_y == 2 else y_in[step, 1]
        along = jnp.concatenate([below, source[...], above], axis=2)
        for offset in range(1, WIDTH + 1):
            local = local + (-0.5 * stencil_terms[offset]) * (
                along[:, :, cy + offset:2 * cy + offset] + along[:, :, cy - offset:2 * cy - offset]
            )

        for copy in coef_copies:
            copy.wait_recv()
        around = jnp.concatenate(
            [coefficients]
            + [coef_in[step, n] for n in range(1, blocks)]
            + [jnp.zeros((seg_rows - 8 * blocks, 128), F32)],
            axis=0,
        )
        high, low = split_two(around.T[0:nproj * norb])
        spread = jnp.dot(
            jnp.concatenate([high, low], axis=0), seg_hot[...], preferred_element_type=F32
        )
        spread = spread[0:nproj * norb] + spread[nproj * norb:2 * nproj * norb]
        returned = spread[0:norb] * masked[0:1, :]
        for j in range(1, nproj):
            returned = returned + spread[j * norb:(j + 1) * norb] * masked[j:j + 1, :]
        high, low = split_two(returned)
        high, low = high.astype(F32), low.astype(F32)
        scattered = jnp.zeros((norb * rows, cz), F32)
        for begin in range(0, points, CHUNK):
            span = slice(begin, begin + CHUNK)
            for term in (high, low):
                spots = (term[:, None, span] * row_hot[:, span][None]).astype(BF16)
                scattered = scattered + lax.dot_general(
                    spots.reshape(norb * rows, CHUNK),
                    lane_hot[0:cz, span],
                    (((1,), (1,)), ((), ())),
                    preferred_element_type=F32,
                )
        scale, keep = factors[step]
        result = scale * (local + scattered.reshape(norb, cx, cy, cz))
        if step > 0:
            previous = orb_ref if step == 1 else field.at[step - 2]
            result = result + keep * previous[...]
        if step < DEGREE - 1:
            field[step] = result
        else:
            out_ref[...] = result

    for copy in started:
        copy.wait_send()


def body(sizes, orbitals, potential, proj_values, point_cell, point_owner, point_slot, point_count, atom_energy):
    norb, cx, cy, cz = orbitals.shape
    nproj, points = proj_values.shape
    rows = cx * cy
    blocks = 1
    for size in sizes:
        blocks = blocks * min(3, size)
    seg_rows = (8 * blocks + 127) // 128 * 128
    copies = 6 + 2 * blocks
    vmem = pl.BlockSpec(memory_space=pltpu.VMEM)
    smem = pl.BlockSpec(memory_space=pltpu.SMEM)
    return pl.pallas_call(
        functools.partial(kernel, sizes),
        out_shape=jax.ShapeDtypeStruct(orbitals.shape, F32),
        in_specs=[vmem] * 6 + [smem, vmem],
        out_specs=vmem,
        scratch_shapes=[
            pltpu.VMEM((DEGREE - 1, norb, cx, cy, cz), F32),
            pltpu.VMEM((DEGREE, norb, WIDTH, cy, cz), F32),
            pltpu.VMEM((DEGREE, norb, WIDTH, cy, cz), F32),
            pltpu.VMEM((DEGREE, 1 if sizes[1] == 2 else 2, norb, cx, cy, cz), F32),
            pltpu.VMEM((DEGREE, 2, 8, norb * rows), F32),
            pltpu.VMEM((DEGREE, 2, 8, norb * rows), F32),
            pltpu.VMEM((DEGREE, blocks, 8, 128), F32),
            pltpu.VMEM((DEGREE, blocks, 8, 128), F32),
            pltpu.VMEM((DEGREE, 8, 128), F32),
            pltpu.VMEM((DEGREE, blocks, 8, 128), F32),
            pltpu.VMEM((2 * cz, points), BF16),
            pltpu.VMEM((rows, points), F32),
            pltpu.VMEM((seg_rows, points), BF16),
            pltpu.VMEM((nproj, points), F32),
            pltpu.SemaphoreType.DMA((DEGREE, copies)),
            pltpu.SemaphoreType.DMA((DEGREE, copies)),
        ],
        compiler_params=pltpu.CompilerParams(
            collective_id=0, has_side_effects=True, vmem_limit_bytes=48 * 1024 * 1024
        ),
    )(
        orbitals,
        potential,
        proj_values,
        point_cell.reshape(1, points),
        point_owner.reshape(1, points),
        point_slot.reshape(1, points),
        point_count,
        atom_energy,
    )


def solution(mesh):
    sizes = tuple(mesh.shape[name] for name in ("gx", "gy", "gz"))
    return jax.shard_map(
        functools.partial(body, sizes),
        mesh=mesh,
        in_specs=(
            P(None, "gx", "gy", "gz"),
            P("gx", "gy", "gz"),
            P(None, ("gx", "gy", "gz")),
            P(("gx", "gy", "gz")),
            P(("gx", "gy", "gz")),
            P(("gx", "gy", "gz")),
            P(("gx", "gy", "gz")),
            P(),
        ),
        out_specs=P(None, "gx", "gy", "gz"),
        check_vma=False,
    )
```

time: 424 us -> 61.6 us (0.15); the launches traced: 417 us -> 61.2 us
  other arithmetic: 142 us -> 0 us
  local copies, waits for them, and re-layouts: 146 us -> 5.28 us
  waiting for transfers between devices: 74 us -> 0 us
  Pallas kernels: 0 us -> 55.3 us
  starting transfers between devices: 54.1 us -> 0 us
    scatter-add x6 -> x0, other arithmetic: 76.9 us -> none  [the longest x3 42.1 us: nonlocal_part(): jnp.zeros_like(flattened).at[:, point_cell].add(returned.T)]
    ppermute x54 -> x0, waiting for transfers between devices: 74 us -> none  [the longest x18 31.5 us: with_halo(): lax.ppermute(tail, axis, [(i, (i + 1) % count) for i in range(count)])]
    gather x9 -> x0, local copies, waits for them, and re-layouts: 72.9 us -> none  [the longest x3 45.8 us: nonlocal_part(): neighbourhood.reshape(27 * ATOM_DEV, projector_count, orbital_count)]
    pallas_call x0 -> x1, Pallas kernels: none -> 55.3 us  [body(): pl.pallas_call(functools.partial(kernel, sizes), out_shape=jax.ShapeDtype...]
    ppermute x54 -> x0, starting transfers between devices: 54.1 us -> none  [the longest x18 22 us: with_halo(): lax.ppermute(head, axis, [((i + 1) % count, i) for i in range(count)])]
    reduce_sum x3 -> x0, other arithmetic: 40 us -> none  [nonlocal_part(): returned = jnp.sum(masked_rows[:, :, None] * atom_rows, axis=1)]
    slice x21 -> x0, local copies, waits for them, and re-layouts: 28.4 us -> none  [the longest x9 15.1 us: with_halo(): head = lax.slice_in_dim(cells, 0, width, axis=dim)]
    ppermute x6 -> x0, local copies, waits for them, and re-layouts: 18.6 us -> none  [the longest x3 9.86 us: with_halo(): lax.ppermute(head, axis, [((i + 1) % count, i) for i in range(count)])]
  transfers between devices with their start and end apart: 54 -> 0, of which waited for: 37 -> 0; matrix products, arithmetic and copies ran while one was open for 39% -> 0% of each run, Pallas kernels for 0% -> 0%
where the time goes in v1:
time: 61.6 us; the launch traced here: 61.2 us
  Pallas kernels  55.3 us (90%)
  local copies, waits for them, and re-layouts  5.28 us (9%)
  between operations  0.68 us (1%)
    pallas_call x1, Pallas kernels, body(): pl.pallas_call(functools.partial(kernel, sizes), out_shape=jax.ShapeDtype...  55.3 us
    unnamed x15, local copies, waits for them, and re-layouts  5.28 us

profile of v1, /device:TPU:0, one launch (start us, length us, event | category | flops | bytes accessed | tf_op | source)
XLA Modules:
  0.0 61.2 jit_solution(88959608246988976)
XLA Ops:
  0.0 0.0 copy-start.6
  0.7 0.0 copy-done.6
  0.7 0.0 copy-start
  0.7 0.9 %copy-done = f32[8,8,8,128]{3,2,1,0:T(8,128)S(1)} copy-done((f32[8,8,8,128]{3,2,1,0:T(8,128)S(1)}, f32[8,8,8,128]{3,2,1,0:T(8,128)}, u32[]{:S(2)}) %copy-start) | copy-done | bytes 262168
  1.6 0.0 copy-start.1
  1.6 0.8 %copy-done.1 = f32[8,8,128]{2,1,0:T(8,128)S(1)} copy-done((f32[8,8,128]{2,1,0:T(8,128)S(1)}, f32[8,8,128]{2,1,0:T(8,128)}, u32[]{:S(2)}) %copy-start.1) | copy-done | bytes 32792
  2.4 0.0 copy-start.2
  2.4 0.8 %copy-done.2 = f32[4,2048]{1,0:T(4,128)S(1)} copy-done((f32[4,2048]{1,0:T(4,128)S(1)}, f32[4,2048]{1,0:T(4,128)}, u32[]{:S(2)}) %copy-start.2) | copy-done | bytes 32792
  3.2 0.0 copy-start.3
  3.2 0.7 %copy-done.3 = s32[2048]{0:T(1024)S(1)} copy-done((s32[2048]{0:T(1024)S(1)}, s32[2048]{0:T(1024)}, u32[]{:S(2)}) %copy-start.3) | copy-done | bytes 8216
  3.9 0.0 copy-start.4
  3.9 0.7 %copy-done.4 = s32[2048]{0:T(1024)S(1)} copy-done((s32[2048]{0:T(1024)S(1)}, s32[2048]{0:T(1024)}, u32[]{:S(2)}) %copy-start.4) | copy-done | bytes 8216
  4.5 0.0 copy-start.5
  4.6 0.7 %copy-done.5 = s32[2048]{0:T(1024)S(1)} copy-done((s32[2048]{0:T(1024)S(1)}, s32[2048]{0:T(1024)}, u32[]{:S(2)}) %copy-start.5) | copy-done | bytes 8216
  5.2 55.3 %shard_map.82 = f32[8,8,8,128]{3,2,1,0:T(8,128)S(1)} custom-call(f32[8,8,8,128]{3,2,1,0:T(8,128)S(1)} %copy-done, f32[8,8,128]{2,1,0:T(8,128)S(1)} %copy-done.1, f32[4,2048]{1,0:T(4,128)S(1)} %copy-done.2, s32[1,2048]{1,0:T(1,128)S(1)} %bitcast.3, s32[1,2048]{1,0:T(1,128)S(1)} %bitcast.4, s32[1,2048]{1,0:T(1,128)S(1)} %bitcast.5, s32[1]{0:T(128)S(6)} %copy.10.count_ref, ...), custom_call_target="tpu_custom_call" | custom-call | tf_op jit(solution)/shard_map/pallas_call | solution.py:296
  60.5 0.7 %copy.11 = f32[8,8,8,128]{3,2,1,0:T(8,128)} copy(f32[8,8,8,128]{3,2,1,0:T(8,128)S(1)} %shard_map.82) | data formatting | bytes 524288
Async XLA Ops:
  0.0 0.7 %copy-start.6 = (f32[4,160]{1,0:T(4,128)S(1)}, f32[4,160]{1,0:T(4,128)}, u32[]{:S(2)}) copy-start(f32[4,160]{1,0:T(4,128)} %energy_ref.1) | copy-start | bytes 7684
  0.7 0.9 %copy-start = (f32[8,8,8,128]{3,2,1,0:T(8,128)S(1)}, f32[8,8,8,128]{3,2,1,0:T(8,128)}, u32[]{:S(2)}) copy-start(f32[8,8,8,128]{3,2,1,0:T(8,128)} %orb_ref.1) | copy-start | bytes 786436
  1.6 0.8 %copy-start.1 = (f32[8,8,128]{2,1,0:T(8,128)S(1)}, f32[8,8,128]{2,1,0:T(8,128)}, u32[]{:S(2)}) copy-start(f32[8,8,128]{2,1,0:T(8,128)} %pot_ref.1) | copy-start | bytes 98308
  2.4 0.8 %copy-start.2 = (f32[4,2048]{1,0:T(4,128)S(1)}, f32[4,2048]{1,0:T(4,128)}, u32[]{:S(2)}) copy-start(f32[4,2048]{1,0:T(4,128)} %val_ref.1) | copy-start | bytes 98308
  3.2 0.7 %copy-start.3 = (s32[2048]{0:T(1024)S(1)}, s32[2048]{0:T(1024)}, u32[]{:S(2)}) copy-start(s32[2048]{0:T(1024)} %param.11) | copy-start | bytes 24580
  3.9 0.7 %copy-start.4 = (s32[2048]{0:T(1024)S(1)}, s32[2048]{0:T(1024)}, u32[]{:S(2)}) copy-start(s32[2048]{0:T(1024)} %param.12) | copy-start | bytes 24580
  4.5 0.7 %copy-start.5 = (s32[2048]{0:T(1024)S(1)}, s32[2048]{0:T(1024)}, u32[]{:S(2)}) copy-start(s32[2048]{0:T(1024)} %param.13) | copy-start | bytes 24580

commit v2 on v1

v2 whole, which is shorter than its diff:
```python
import functools

import jax
import jax.numpy as jnp
from jax import lax
from jax.experimental import pallas as pl
from jax.experimental.pallas import tpu as pltpu
from jax.sharding import PartitionSpec as P

DEGREE = 3
ATOM_DEV = 5
WIDTH = 6
CHUNK = 512
GROUPS = 1
MESH = pl.DeviceIdType.MESH
F32 = jnp.float32
BF16 = jnp.bfloat16

stencil_terms = (
    -5369.0 / 1800.0,
    12.0 / 7.0,
    -15.0 / 56.0,
    10.0 / 189.0,
    -1.0 / 112.0,
    2.0 / 1925.0,
    -1.0 / 16632.0,
)
lowest = -3.5
cutoff = 1.5
highest = 13.0


def step_factors():
    half = (highest - cutoff) / 2.0
    middle = (highest + cutoff) / 2.0
    first = half / (lowest - middle)
    factors = [(first / half, 0.0)]
    sigma = first
    for _ in range(1, DEGREE):
        following = 1.0 / (2.0 / first - sigma)
        factors.append((2.0 * following / half, -sigma * following))
        sigma = following
    return middle, factors


def split_two(value):
    high = value.astype(BF16)
    low = (value - high.astype(F32)).astype(BF16)
    return high, low


def by_distance(distance):
    result = jnp.zeros(distance.shape, F32)
    for offset in range(WIDTH + 1):
        weight = 0.0 if offset == 0 else -0.5 * stencil_terms[offset]
        result = jnp.where(jnp.abs(distance) == offset, weight, result)
    return result


def kernel(
    sizes, groups,
    orb_hbm, pot_hbm, val_hbm, cell_hbm, owner_hbm, slot_hbm, count_ref, energy_hbm,
    out_ref,
    orb_ref, pot_ref, val_ref, cell_ref, owner_ref, slot_ref, energy_ref,
    field, acc, x_low, x_high, y_in, z_out, z_in, part_out, part_in, coef_out, coef_in,
    lane_hot, row_hot, seg_hot, masked, load_sem, send_sem, recv_sem,
):
    size_x, size_y, size_z = sizes
    norb, cx, cy, cz = orb_ref.shape
    nproj, points = val_ref.shape
    rows = cx * cy
    each = norb // groups
    spans = [min(3, size) for size in sizes]
    codes = [(a, b, c) for a in range(spans[0]) for b in range(spans[1]) for c in range(spans[2])]
    blocks = len(codes)
    seg_rows = seg_hot.shape[0]
    here = [lax.axis_index(name) for name in ("gx", "gy", "gz")]
    names = ("gx", "gy", "gz")

    loads = [
        pltpu.make_async_copy(source, target, load_sem.at[n])
        for n, (source, target) in enumerate(
            [
                (orb_hbm, orb_ref),
                (cell_hbm, cell_ref),
                (owner_hbm, owner_ref),
                (slot_hbm, slot_ref),
                (val_hbm, val_ref),
                (energy_hbm, energy_ref),
                (pot_hbm, pot_ref),
            ]
        )
    ]
    for load in loads:
        load.start()

    def moved(axis, code):
        step = (0, 1, sizes[axis] - 1)[code]
        return lax.rem(here[axis] + step, sizes[axis])

    def device(code):
        return {name: moved(axis, code[axis]) for axis, name in enumerate(names)}

    def opposite(code):
        back = [0 if c == 0 else (1 if sizes[a] == 2 else 3 - c) for a, c in enumerate(code)]
        return codes.index(tuple(back))

    up = [{names[axis]: moved(axis, 1)} for axis in range(3)]
    down = [{names[axis]: lax.rem(here[axis] + sizes[axis] - 1, sizes[axis])} for axis in range(3)]

    barrier = pltpu.get_barrier_semaphore()
    for code in codes[1:]:
        pl.semaphore_signal(barrier, inc=1, device_id=device(code), device_id_type=MESH)

    middle, factors = step_factors()
    started = []

    def send(step, group, index, source, target, device_id):
        copy = pltpu.make_async_remote_copy(
            src_ref=source,
            dst_ref=target,
            send_sem=send_sem.at[step, group, index],
            recv_sem=recv_sem.at[step, group, index],
            device_id=device_id,
            device_id_type=MESH,
        )
        copy.start()
        started.append(copy)
        return copy

    def source_of(step):
        return orb_ref if step == 0 else field.at[step - 1]

    state = {}

    def send_faces(step, group):
        span = pl.ds(group * each, each)
        source = source_of(step)
        y_copies = [
            send(step, group, 2, source.at[span], y_in.at[step, 0, span], up[1])
        ]
        if size_y > 2:
            y_copies.append(send(step, group, 3, source.at[span], y_in.at[step, 1, span], down[1]))
        x_copies = [
            send(
                step, group, 0, source.at[span, pl.ds(cx - WIDTH, WIDTH)], x_low.at[step, span], up[0]
            ),
            send(step, group, 1, source.at[span, pl.ds(0, WIDTH)], x_high.at[step, span], down[0]),
        ]
        state[step, group] = {"x": x_copies, "y": y_copies}

    first = lax.broadcasted_iota(jnp.int32, (cz, cz), 0)
    second = lax.broadcasted_iota(jnp.int32, (cz, cz), 1)
    high, low = split_two(by_distance(first - second))
    band = jnp.concatenate(
        [
            jnp.concatenate([high, low], axis=1),
            jnp.concatenate([high, jnp.zeros_like(low)], axis=1),
        ],
        axis=0,
    )
    place = lax.broadcasted_iota(jnp.int32, (16, cz), 0)
    lane = lax.broadcasted_iota(jnp.int32, (16, cz), 1)
    high, low = split_two(by_distance(jnp.where(place < 8, place - 8, place - 8 + cz) - lane))
    edge_band = jnp.concatenate([high, high, low], axis=0)
    edge_pick = (lane == jnp.where(place < 8, place, place - 16 + cz)).astype(F32).astype(BF16)
    edge_pick = jnp.concatenate([edge_pick, edge_pick], axis=1)

    pl.semaphore_wait(barrier, blocks - 1)
    loads[0].wait()
    for group in range(groups):
        send_faces(0, group)

    for load in loads[1:]:
        load.wait()
    cells = cell_ref[...]
    lanes_of = cells % cz
    rows_of = cells // cz
    at_lane = (lax.broadcasted_iota(jnp.int32, (cz, points), 0) == lanes_of).astype(F32).astype(BF16)
    lane_hot[0:cz, :] = at_lane
    lane_hot[cz:2 * cz, :] = at_lane
    row_hot[...] = (lax.broadcasted_iota(jnp.int32, (rows, points), 0) == rows_of).astype(F32)
    owner = owner_ref[...]
    coords = (owner // (size_y * size_z), owner // size_z % size_y, owner % size_z)
    block = jnp.zeros_like(owner)
    for axis in range(3):
        remain = (coords[axis] - here[axis] + sizes[axis]) % sizes[axis]
        block = block * spans[axis] + jnp.minimum(remain, 2)
    segment = block * 8 + slot_ref[...]
    seg_hot[...] = (
        lax.broadcasted_iota(jnp.int32, (seg_rows, points), 0) == segment
    ).astype(F32).astype(BF16)
    live = lax.broadcasted_iota(jnp.int32, (nproj, points), 1) < count_ref[0]
    masked[...] = jnp.where(live, val_ref[...], 0.0)

    atoms = energy_ref.shape[1]
    domain = (here[0] * size_y + here[1]) * size_z + here[2]
    slots = lax.broadcasted_iota(jnp.int32, (8, atoms), 0)
    mine = (lax.broadcasted_iota(jnp.int32, (8, atoms), 1) == domain * ATOM_DEV + slots) & (
        slots < ATOM_DEV
    )
    lane_group = lax.broadcasted_iota(jnp.int32, (8, 128), 1) // each
    energies = jnp.zeros((8, 128), F32)
    for j in range(nproj):
        own = jnp.sum(jnp.where(mine, energy_ref[j:j + 1, :], 0.0), axis=1, keepdims=True)
        energies = jnp.where(lane_group == j, own, energies)

    used = nproj * each

    def begin(step, group):
        now = state[step, group]
        span = slice(group * each, group * each + each)
        flat = source_of(step)[span].reshape(each * rows, cz)
        high, low = split_two(flat)
        both = jnp.concatenate([high, low], axis=1)
        now["both"] = both
        z_out[step, group] = lax.dot_general(
            edge_pick, both, (((1,), (1,)), ((), ())), preferred_element_type=F32
        ).reshape(2, 8, each * rows)
        now["z"] = [
            send(step, group, 4, z_out.at[step, group, 1], z_in.at[step, group, 0], up[2]),
            send(step, group, 5, z_out.at[step, group, 0], z_in.at[step, group, 1], down[2]),
        ]
        weighted = []
        for start in range(0, points, CHUNK):
            part = slice(start, start + CHUNK)
            spread = jnp.dot(both, lane_hot[:, part], preferred_element_type=F32)
            sampled = jnp.sum(spread.reshape(each, rows, CHUNK) * row_hot[:, part][None], axis=1)
            weighted.append(
                jnp.concatenate([sampled * masked[j:j + 1, part] for j in range(nproj)], axis=0)
            )
        high, low = split_two(jnp.concatenate(weighted, axis=1))
        filler = jnp.zeros((128 - 2 * used, points), BF16)
        partial = lax.dot_general(
            seg_hot[...],
            jnp.concatenate([high, low, filler], axis=0),
            (((1,), (1,)), ((), ())),
            preferred_element_type=F32,
        )
        partial = partial + pltpu.roll(partial, 128 - used, 1)
        now["own"] = partial[0:8]
        part_out[step, group] = partial[0:blocks * 8].reshape(blocks, 8, 128)
        now["part"] = [
            send(
                step, group, 6 + n, part_out.at[step, group, n], part_in.at[step, group, n],
                device(codes[n]),
            )
            for n in range(1, blocks)
        ]

    def along_lanes(step, group):
        now = state[step, group]
        span = slice(group * each, group * each + each)
        total = jnp.dot(now["both"], band, preferred_element_type=F32)
        total = total[:, 0:cz] + total[:, cz:2 * cz]
        for copy in now["z"]:
            copy.wait_recv()
        high, low = split_two(z_in[step, group].reshape(16, each * rows))
        edges = jnp.concatenate([high.astype(F32), low.astype(F32), high.astype(F32)], axis=0)
        total = total + jnp.dot(edges.T.astype(BF16), edge_band, preferred_element_type=F32)
        acc[span] = total.reshape(each, cx, cy, cz)

    def give_back(step, group):
        now = state[step, group]
        owned = now["own"]
        for n, copy in enumerate(now["part"], 1):
            copy.wait_recv()
            owned = owned + part_in[step, group, n]
        coefficients = owned * energies
        now["own"] = coefficients
        coef_out[step, group] = coefficients
        now["coef"] = [
            send(
                step, group, 6 + blocks + n, coef_out.at[step, group],
                coef_in.at[step, group, opposite(codes[n])], device(codes[n]),
            )
            for n in range(1, blocks)
        ]

    def across_rows(step, group):
        now = state[step, group]
        for copy in now["x"] + now["y"]:
            copy.wait_recv()
        source = source_of(step)
        for o in range(group * each, group * each + each):
            own = source[o]
            total = acc[o] + (pot_ref[...] + (-1.5 * stencil_terms[0] - middle)) * own
            below = y_in[step, 0, o]
            above = below if size_y == 2 else y_in[step, 1, o]
            in_x = jnp.concatenate([x_low[step, o], own, x_high[step, o]], axis=0)
            in_y = jnp.concatenate([below, own, above], axis=1)
            for k in range(1, WIDTH + 1):
                total = total + (-0.5 * stencil_terms[k]) * (
                    (in_x[WIDTH + k:WIDTH + k + cx] + in_x[WIDTH - k:WIDTH - k + cx])
                    + (in_y[:, cy + k:2 * cy + k] + in_y[:, cy - k:2 * cy - k])
                )
            acc[o] = total

    def finish(step, group):
        now = state[step, group]
        for copy in now["coef"]:
            copy.wait_recv()
        around = jnp.concatenate(
            [now["own"]]
            + [coef_in[step, group, n] for n in range(1, blocks)]
            + [jnp.zeros((seg_rows - 8 * blocks, 128), F32)],
            axis=0,
        )
        high, low = split_two(around.T[0:used])
        spread = jnp.dot(
            jnp.concatenate([high, low], axis=0), seg_hot[...], preferred_element_type=F32
        )
        spread = spread[0:used] + spread[used:2 * used]
        returned = spread[0:each] * masked[0:1, :]
        for j in range(1, nproj):
            returned = returned + spread[j * each:(j + 1) * each] * masked[j:j + 1, :]
        high, low = split_two(returned)
        high, low = high.astype(F32), low.astype(F32)
        scattered = jnp.zeros((each * rows, cz), F32)
        for start in range(0, points, CHUNK):
            part = slice(start, start + CHUNK)
            at_row = row_hot[:, part].astype(BF16).reshape(1, rows // 16, 16, CHUNK)
            for term in (high, low):
                wide = jnp.broadcast_to(term[:, None, part], (each, 16, CHUNK)).astype(BF16)
                spots = wide[:, None] * at_row
                scattered = scattered + lax.dot_general(
                    spots.reshape(each * rows, CHUNK),
                    lane_hot[0:cz, part],
                    (((1,), (1,)), ((), ())),
                    preferred_element_type=F32,
                )
        scattered = scattered.reshape(each, cx, cy, cz)
        scale, keep = factors[step]
        span = slice(group * each, group * each + each)
        result = scale * (acc[span] + scattered)
        if step > 0:
            result = result + keep * source_of(step - 1)[span]
        if step < DEGREE - 1:
            field[step, span] = result
        else:
            out_ref[span] = result

    everyone = range(groups)
    for group in everyone:
        begin(0, group)
    for step in range(DEGREE):
        for group in everyone:
            along_lanes(step, group)
            give_back(step, group)
        for group in everyone:
            across_rows(step, group)
            finish(step, group)
            if step < DEGREE - 1:
                send_faces(step + 1, group)
                begin(step + 1, group)

    for copy in started:
        copy.wait_send()


def body(sizes, orbitals, potential, proj_values, point_cell, point_owner, point_slot, point_count, atom_energy):
    norb, cx, cy, cz = orbitals.shape
    nproj, points = proj_values.shape
    rows = cx * cy
    blocks = 1
    for size in sizes:
        blocks = blocks * min(3, size)
    seg_rows = (8 * blocks + 127) // 128 * 128
    copies = 6 + 2 * blocks
    groups = GROUPS
    each_rows = norb // groups * rows
    vmem = pl.BlockSpec(memory_space=pltpu.VMEM)
    smem = pl.BlockSpec(memory_space=pltpu.SMEM)
    hbm = pl.BlockSpec(memory_space=pltpu.HBM)
    return pl.pallas_call(
        functools.partial(kernel, sizes, groups),
        out_shape=jax.ShapeDtypeStruct(orbitals.shape, F32),
        in_specs=[hbm] * 6 + [smem, hbm],
        out_specs=vmem,
        scratch_shapes=[
            pltpu.VMEM(orbitals.shape, F32),
            pltpu.VMEM(potential.shape, F32),
            pltpu.VMEM(proj_values.shape, F32),
            pltpu.VMEM((1, points), jnp.int32),
            pltpu.VMEM((1, points), jnp.int32),
            pltpu.VMEM((1, points), jnp.int32),
            pltpu.VMEM(atom_energy.shape, F32),
            pltpu.VMEM((DEGREE - 1, norb, cx, cy, cz), F32),
            pltpu.VMEM((norb, cx, cy, cz), F32),
            pltpu.VMEM((DEGREE, norb, WIDTH, cy, cz), F32),
            pltpu.VMEM((DEGREE, norb, WIDTH, cy, cz), F32),
            pltpu.VMEM((DEGREE, 1 if sizes[1] == 2 else 2, norb, cx, cy, cz), F32),
            pltpu.VMEM((DEGREE, groups, 2, 8, each_rows), F32),
            pltpu.VMEM((DEGREE, groups, 2, 8, each_rows), F32),
            pltpu.VMEM((DEGREE, groups, blocks, 8, 128), F32),
            pltpu.VMEM((DEGREE, groups, blocks, 8, 128), F32),
            pltpu.VMEM((DEGREE, groups, 8, 128), F32),
            pltpu.VMEM((DEGREE, groups, blocks, 8, 128), F32),
            pltpu.VMEM((2 * cz, points), BF16),
            pltpu.VMEM((rows, points), F32),
            pltpu.VMEM((seg_rows, points), BF16),
            pltpu.VMEM((nproj, points), F32),
            pltpu.SemaphoreType.DMA((7,)),
            pltpu.SemaphoreType.DMA((DEGREE, groups, copies)),
            pltpu.SemaphoreType.DMA((DEGREE, groups, copies)),
        ],
        compiler_params=pltpu.CompilerParams(
            collective_id=0, has_side_effects=True, vmem_limit_bytes=48 * 1024 * 1024
        ),
    )(
        orbitals,
        potential,
        proj_values,
        point_cell.reshape(1, points),
        point_owner.reshape(1, points),
        point_slot.reshape(1, points),
        point_count,
        atom_energy,
    )


def solution(mesh):
    sizes = tuple(mesh.shape[name] for name in ("gx", "gy", "gz"))
    return jax.shard_map(
        functools.partial(body, sizes),
        mesh=mesh,
        in_specs=(
            P(None, "gx", "gy", "gz"),
            P("gx", "gy", "gz"),
            P(None, ("gx", "gy", "gz")),
            P(("gx", "gy", "gz")),
            P(("gx", "gy", "gz")),
            P(("gx", "gy", "gz")),
            P(("gx", "gy", "gz")),
            P(),
        ),
        out_specs=P(None, "gx", "gy", "gz"),
        check_vma=False,
    )
```

time: 61.6 us -> 61.9 us (level)
  no operation moved by 1% of the time
where the time goes in v2:
time: 61.9 us; the launch traced here: 61.5 us
  Pallas kernels  55.5 us (90%)
  local copies, waits for them, and re-layouts  5.28 us (9%)
  between operations  0.68 us (1%)
    pallas_call x1, Pallas kernels, body(): pl.pallas_call(functools.partial(kernel, sizes, groups), out_shape=jax.Sh...  55.5 us
    unnamed x15, local copies, waits for them, and re-layouts  5.28 us

profile of v2, /device:TPU:0, one launch (start us, length us, event | category | flops | bytes accessed | tf_op | source)
XLA Modules:
  0.0 61.5 jit_solution(13662569638139497626)
XLA Ops:
  0.0 0.0 copy-start.6
  0.7 0.0 copy-done.6
  0.7 0.0 copy-start
  0.7 0.9 %copy-done = f32[8,8,8,128]{3,2,1,0:T(8,128)S(1)} copy-done((f32[8,8,8,128]{3,2,1,0:T(8,128)S(1)}, f32[8,8,8,128]{3,2,1,0:T(8,128)}, u32[]{:S(2)}) %copy-start) | copy-done | bytes 262168
  1.6 0.0 copy-start.1
  1.6 0.8 %copy-done.1 = f32[8,8,128]{2,1,0:T(8,128)S(1)} copy-done((f32[8,8,128]{2,1,0:T(8,128)S(1)}, f32[8,8,128]{2,1,0:T(8,128)}, u32[]{:S(2)}) %copy-start.1) | copy-done | bytes 32792
  2.4 0.0 copy-start.2
  2.4 0.8 %copy-done.2 = f32[4,2048]{1,0:T(4,128)S(1)} copy-done((f32[4,2048]{1,0:T(4,128)S(1)}, f32[4,2048]{1,0:T(4,128)}, u32[]{:S(2)}) %copy-start.2) | copy-done | bytes 32792
  3.2 0.0 copy-start.3
  3.2 0.7 %copy-done.3 = s32[2048]{0:T(1024)S(1)} copy-done((s32[2048]{0:T(1024)S(1)}, s32[2048]{0:T(1024)}, u32[]{:S(2)}) %copy-start.3) | copy-done | bytes 8216
  3.9 0.0 copy-start.4
  3.9 0.7 %copy-done.4 = s32[2048]{0:T(1024)S(1)} copy-done((s32[2048]{0:T(1024)S(1)}, s32[2048]{0:T(1024)}, u32[]{:S(2)}) %copy-start.4) | copy-done | bytes 8216
  4.5 0.0 copy-start.5
  4.6 0.7 %copy-done.5 = s32[2048]{0:T(1024)S(1)} copy-done((s32[2048]{0:T(1024)S(1)}, s32[2048]{0:T(1024)}, u32[]{:S(2)}) %copy-start.5) | copy-done | bytes 8216
  5.2 55.5 %shard_map.82 = f32[8,8,8,128]{3,2,1,0:T(8,128)S(1)} custom-call(f32[8,8,8,128]{3,2,1,0:T(8,128)S(1)} %copy-done, f32[8,8,128]{2,1,0:T(8,128)S(1)} %copy-done.1, f32[4,2048]{1,0:T(4,128)S(1)} %copy-done.2, s32[1,2048]{1,0:T(1,128)S(1)} %bitcast.3, s32[1,2048]{1,0:T(1,128)S(1)} %bitcast.4, s32[1,2048]{1,0:T(1,128)S(1)} %bitcast.5, s32[1]{0:T(128)S(6)} %copy.10.count_ref, ...), custom_call_target="tpu_custom_call" | custom-call | tf_op jit(solution)/shard_map/pallas_call | solution.py:375
  60.7 0.7 %copy.11 = f32[8,8,8,128]{3,2,1,0:T(8,128)} copy(f32[8,8,8,128]{3,2,1,0:T(8,128)S(1)} %shard_map.82) | data formatting | bytes 524288
Async XLA Ops:
  0.0 0.7 %copy-start.6 = (f32[4,160]{1,0:T(4,128)S(1)}, f32[4,160]{1,0:T(4,128)}, u32[]{:S(2)}) copy-start(f32[4,160]{1,0:T(4,128)} %energy_hbm.1) | copy-start | bytes 7684
  0.7 0.9 %copy-start = (f32[8,8,8,128]{3,2,1,0:T(8,128)S(1)}, f32[8,8,8,128]{3,2,1,0:T(8,128)}, u32[]{:S(2)}) copy-start(f32[8,8,8,128]{3,2,1,0:T(8,128)} %orb_hbm.1) | copy-start | bytes 786436
  1.6 0.8 %copy-start.1 = (f32[8,8,128]{2,1,0:T(8,128)S(1)}, f32[8,8,128]{2,1,0:T(8,128)}, u32[]{:S(2)}) copy-start(f32[8,8,128]{2,1,0:T(8,128)} %pot_hbm.1) | copy-start | bytes 98308
  2.4 0.8 %copy-start.2 = (f32[4,2048]{1,0:T(4,128)S(1)}, f32[4,2048]{1,0:T(4,128)}, u32[]{:S(2)}) copy-start(f32[4,2048]{1,0:T(4,128)} %val_hbm.1) | copy-start | bytes 98308
  3.2 0.7 %copy-start.3 = (s32[2048]{0:T(1024)S(1)}, s32[2048]{0:T(1024)}, u32[]{:S(2)}) copy-start(s32[2048]{0:T(1024)} %param.11) | copy-start | bytes 24580
  3.9 0.7 %copy-start.4 = (s32[2048]{0:T(1024)S(1)}, s32[2048]{0:T(1024)}, u32[]{:S(2)}) copy-start(s32[2048]{0:T(1024)} %param.12) | copy-start | bytes 24580
  4.5 0.7 %copy-start.5 = (s32[2048]{0:T(1024)S(1)}, s32[2048]{0:T(1024)}, u32[]{:S(2)}) copy-start(s32[2048]{0:T(1024)} %param.13) | copy-start | bytes 24580

commit v3 on v2

--- a/solution.py
+++ b/solution.py
@@ -11,7 +11,7 @@
 ATOM_DEV = 5
 WIDTH = 6
 CHUNK = 512
-GROUPS = 1
+GROUPS = 2
 MESH = pl.DeviceIdType.MESH
 F32 = jnp.float32
 BF16 = jnp.bfloat16
@@ -405,7 +405,7 @@
             pltpu.SemaphoreType.DMA((DEGREE, groups, copies)),
         ],
         compiler_params=pltpu.CompilerParams(
-            collective_id=0, has_side_effects=True, vmem_limit_bytes=48 * 1024 * 1024
+            collective_id=0, has_side_effects=True, vmem_limit_bytes=63 * 1024 * 1024
         ),
     )(
         orbitals,

time: 61.9 us -> 58.7 us (0.948)
  local copies, waits for them, and re-layouts: 5.28 us -> 1.67 us
  Pallas kernels: 55.5 us -> 56.2 us
    unnamed x15 -> x1, local copies, waits for them, and re-layouts: 5.28 us -> 1.67 us
    pallas_call x1, Pallas kernels: 55.5 us -> 56.2 us  [body(): pl.pallas_call(functools.partial(kernel, sizes, groups), out_shape=jax.Sh...]
where the time goes in v3:
time: 58.7 us; the launch traced here: 58.5 us
  Pallas kernels  56.2 us (96%)
  local copies, waits for them, and re-layouts  1.67 us (3%)
  between operations  0.66 us (1%)
    pallas_call x1, Pallas kernels, body(): pl.pallas_call(functools.partial(kernel, sizes, groups), out_shape=jax.Sh...  56.2 us
    unnamed x1, local copies, waits for them, and re-layouts  1.67 us

profile of v3, /device:TPU:0, one launch (start us, length us, event | category | flops | bytes accessed | tf_op | source)
XLA Modules:
  0.0 58.5 jit_solution(13837472191082173581)
XLA Ops:
  0.7 56.2 %shard_map.82 = f32[8,8,8,128]{3,2,1,0:T(8,128)} custom-call(f32[8,8,8,128]{3,2,1,0:T(8,128)} %orb_hbm.1, f32[8,8,128]{2,1,0:T(8,128)} %pot_hbm.1, f32[4,2048]{1,0:T(4,128)} %val_hbm.1, s32[1,2048]{1,0:T(1,128)} %bitcast.3, s32[1,2048]{1,0:T(1,128)} %bitcast.4, s32[1,2048]{1,0:T(1,128)} %bitcast.5, s32[1]{0:T(128)S(6)} %copy.10.count_ref, f32[4,160]{1,0:T(4,128)} %energy_hbm.1), custom_call_target="tpu_custom_call" | custom-call | tf_op jit(solution)/shard_map/pallas_call | solution.py:375
  56.8 1.7 %copy.11 = f32[8,8,8,128]{3,2,1,0:T(8,128)} copy(f32[8,8,8,128]{3,2,1,0:T(8,128)} %shard_map.82) | data formatting | bytes 524288

commit v4 on v3

--- a/solution.py
+++ b/solution.py
@@ -10,7 +10,7 @@
 DEGREE = 3
 ATOM_DEV = 5
 WIDTH = 6
-CHUNK = 512
+CHUNK = 256
 GROUPS = 2
 MESH = pl.DeviceIdType.MESH
 F32 = jnp.float32
@@ -49,6 +49,12 @@
     return high, low
 
 
+def divided(value, by):
+    if by & (by - 1):
+        return value // by, value % by
+    return value >> (by.bit_length() - 1), value & (by - 1)
+
+
 def by_distance(distance):
     result = jnp.zeros(distance.shape, F32)
     for offset in range(WIDTH + 1):
@@ -63,7 +69,7 @@
     out_ref,
     orb_ref, pot_ref, val_ref, cell_ref, owner_ref, slot_ref, energy_ref,
     field, acc, x_low, x_high, y_in, z_out, z_in, part_out, part_in, coef_out, coef_in,
-    lane_hot, row_hot, seg_hot, masked, load_sem, send_sem, recv_sem,
+    lane_hot, lane_turn, row_hot, seg_hot, seg_turn, masked, load_sem, send_sem, recv_sem,
 ):
     size_x, size_y, size_z = sizes
     norb, cx, cy, cz = orb_ref.shape
@@ -174,22 +180,24 @@
     for load in loads[1:]:
         load.wait()
     cells = cell_ref[...]
-    lanes_of = cells % cz
-    rows_of = cells // cz
-    at_lane = (lax.broadcasted_iota(jnp.int32, (cz, points), 0) == lanes_of).astype(F32).astype(BF16)
-    lane_hot[0:cz, :] = at_lane
-    lane_hot[cz:2 * cz, :] = at_lane
+    rows_of, lanes_of = divided(cells, cz)
+    at_lane = (lax.broadcasted_iota(jnp.int32, (cz, points), 0) == lanes_of).astype(F32)
+    lane_hot[0:cz, :] = at_lane.astype(BF16)
+    lane_hot[cz:2 * cz, :] = at_lane.astype(BF16)
+    lane_turn[...] = at_lane.T.astype(BF16)
     row_hot[...] = (lax.broadcasted_iota(jnp.int32, (rows, points), 0) == rows_of).astype(F32)
     owner = owner_ref[...]
-    coords = (owner // (size_y * size_z), owner // size_z % size_y, owner % size_z)
+    owner_xy, owner_z = divided(owner, size_z)
+    owner_x, owner_y = divided(owner_xy, size_y)
+    coords = (owner_x, owner_y, owner_z)
     block = jnp.zeros_like(owner)
     for axis in range(3):
-        remain = (coords[axis] - here[axis] + sizes[axis]) % sizes[axis]
+        remain = divided(coords[axis] - here[axis] + sizes[axis], sizes[axis])[1]
         block = block * spans[axis] + jnp.minimum(remain, 2)
     segment = block * 8 + slot_ref[...]
-    seg_hot[...] = (
-        lax.broadcasted_iota(jnp.int32, (seg_rows, points), 0) == segment
-    ).astype(F32).astype(BF16)
+    at_seg = (lax.broadcasted_iota(jnp.int32, (seg_rows, points), 0) == segment).astype(F32)
+    seg_hot[...] = at_seg.astype(BF16)
+    seg_turn[...] = at_seg.T.astype(BF16)
     live = lax.broadcasted_iota(jnp.int32, (nproj, points), 1) < count_ref[0]
     masked[...] = jnp.where(live, val_ref[...], 0.0)
 
@@ -230,14 +238,12 @@
                 jnp.concatenate([sampled * masked[j:j + 1, part] for j in range(nproj)], axis=0)
             )
         high, low = split_two(jnp.concatenate(weighted, axis=1))
-        filler = jnp.zeros((128 - 2 * used, points), BF16)
-        partial = lax.dot_general(
-            seg_hot[...],
-            jnp.concatenate([high, low, filler], axis=0),
-            (((1,), (1,)), ((), ())),
-            preferred_element_type=F32,
+        partial = jnp.dot(
+            jnp.concatenate([high, low], axis=0), seg_turn[...], preferred_element_type=F32
         )
-        partial = partial + pltpu.roll(partial, 128 - used, 1)
+        partial = jnp.concatenate(
+            [partial[0:used] + partial[used:2 * used], jnp.zeros((128 - used, seg_rows), F32)], axis=0
+        ).T
         now["own"] = partial[0:8]
         part_out[step, group] = partial[0:blocks * 8].reshape(blocks, 8, 128)
         now["part"] = [
@@ -320,15 +326,16 @@
         for start in range(0, points, CHUNK):
             part = slice(start, start + CHUNK)
             at_row = row_hot[:, part].astype(BF16).reshape(1, rows // 16, 16, CHUNK)
+            spots = []
             for term in (high, low):
                 wide = jnp.broadcast_to(term[:, None, part], (each, 16, CHUNK)).astype(BF16)
-                spots = wide[:, None] * at_row
-                scattered = scattered + lax.dot_general(
-                    spots.reshape(each * rows, CHUNK),
-                    lane_hot[0:cz, part],
-                    (((1,), (1,)), ((), ())),
-                    preferred_element_type=F32,
-                )
+                spots.append((wide[:, None] * at_row).reshape(each * rows, CHUNK))
+            turned = lane_turn[part]
+            scattered = scattered + jnp.dot(
+                jnp.concatenate(spots, axis=1),
+                jnp.concatenate([turned, turned], axis=0),
+                preferred_element_type=F32,
+            )
         scattered = scattered.reshape(each, cx, cy, cz)
         scale, keep = factors[step]
         span = slice(group * each, group * each + each)
@@ -397,8 +404,10 @@
             pltpu.VMEM((DEGREE, groups, 8, 128), F32),
             pltpu.VMEM((DEGREE, groups, blocks, 8, 128), F32),
             pltpu.VMEM((2 * cz, points), BF16),
+            pltpu.VMEM((points, cz), BF16),
             pltpu.VMEM((rows, points), F32),
             pltpu.VMEM((seg_rows, points), BF16),
+            pltpu.VMEM((points, seg_rows), BF16),
             pltpu.VMEM((nproj, points), F32),
             pltpu.SemaphoreType.DMA((7,)),
             pltpu.SemaphoreType.DMA((DEGREE, groups, copies)),

time: 58.7 us -> 56.3 us (0.959)
  Pallas kernels: 56.2 us -> 53.5 us
    pallas_call x1, Pallas kernels: 56.2 us -> 53.5 us  [body(): pl.pallas_call(functools.partial(kernel, sizes, groups), out_shape=jax.Sh...]
where the time goes in v4:
time: 56.3 us; the launch traced here: 55.9 us
  Pallas kernels  53.5 us (95%)
  local copies, waits for them, and re-layouts  1.67 us (3%)
  between operations  0.66 us (1%)
    pallas_call x1, Pallas kernels, body(): pl.pallas_call(functools.partial(kernel, sizes, groups), out_shape=jax.Sh...  53.5 us
    unnamed x1, local copies, waits for them, and re-layouts  1.67 us

profile of v4, /device:TPU:0, one launch (start us, length us, event | category | flops | bytes accessed | tf_op | source)
XLA Modules:
  0.0 55.9 jit_solution(3957056662982323215)
XLA Ops:
  0.7 53.5 %shard_map.82 = f32[8,8,8,128]{3,2,1,0:T(8,128)} custom-call(f32[8,8,8,128]{3,2,1,0:T(8,128)} %orb_hbm.1, f32[8,8,128]{2,1,0:T(8,128)} %pot_hbm.1, f32[4,2048]{1,0:T(4,128)} %val_hbm.1, s32[1,2048]{1,0:T(1,128)} %bitcast.3, s32[1,2048]{1,0:T(1,128)} %bitcast.4, s32[1,2048]{1,0:T(1,128)} %bitcast.5, s32[1]{0:T(128)S(6)} %copy.10.count_ref, f32[4,160]{1,0:T(4,128)} %energy_hbm.1), custom_call_target="tpu_custom_call" | custom-call | tf_op jit(solution)/shard_map/pallas_call | solution.py:382
  54.2 1.7 %copy.11 = f32[8,8,8,128]{3,2,1,0:T(8,128)} copy(f32[8,8,8,128]{3,2,1,0:T(8,128)} %shard_map.82) | data formatting | bytes 524288

commit v5 on v4

--- a/solution.py
+++ b/solution.py
@@ -66,10 +66,10 @@
 def kernel(
     sizes, groups,
     orb_hbm, pot_hbm, val_hbm, cell_hbm, owner_hbm, slot_hbm, count_ref, energy_hbm,
-    out_ref,
+    out_hbm,
     orb_ref, pot_ref, val_ref, cell_ref, owner_ref, slot_ref, energy_ref,
     field, acc, x_low, x_high, y_in, z_out, z_in, part_out, part_in, coef_out, coef_in,
-    lane_hot, lane_turn, row_hot, seg_hot, seg_turn, masked, load_sem, send_sem, recv_sem,
+    lane_hot, lane_turn, row_hot, seg_hot, seg_turn, masked, load_sem, store_sem, send_sem, recv_sem,
 ):
     size_x, size_y, size_z = sizes
     norb, cx, cy, cz = orb_ref.shape
@@ -100,9 +100,13 @@
     for load in loads:
         load.start()
 
+    places = [
+        [here[axis]] + [lax.rem(here[axis] + step, sizes[axis]) for step in (1, sizes[axis] - 1)]
+        for axis in range(3)
+    ]
+
     def moved(axis, code):
-        step = (0, 1, sizes[axis] - 1)[code]
-        return lax.rem(here[axis] + step, sizes[axis])
+        return places[axis][code]
 
     def device(code):
         return {name: moved(axis, code[axis]) for axis, name in enumerate(names)}
@@ -112,7 +116,7 @@
         return codes.index(tuple(back))
 
     up = [{names[axis]: moved(axis, 1)} for axis in range(3)]
-    down = [{names[axis]: lax.rem(here[axis] + sizes[axis] - 1, sizes[axis])} for axis in range(3)]
+    down = [{names[axis]: moved(axis, 2)} for axis in range(3)]
 
     barrier = pltpu.get_barrier_semaphore()
     for code in codes[1:]:
@@ -120,6 +124,7 @@
 
     middle, factors = step_factors()
     started = []
+    stores = []
 
     def send(step, group, index, source, target, device_id):
         copy = pltpu.make_async_remote_copy(
@@ -131,8 +136,13 @@
             device_id_type=MESH,
         )
         copy.start()
-        started.append(copy)
+        if index < 6:
+            started.append(copy)
         return copy
+
+    def await_tiles(step, group, sems, index):
+        tiles = part_in.at[step, group, pl.ds(1, blocks - 1)]
+        pltpu.make_async_copy(tiles, tiles, sems.at[step, group, index]).wait()
 
     def source_of(step):
         return orb_ref if step == 0 else field.at[step - 1]
@@ -246,13 +256,11 @@
         ).T
         now["own"] = partial[0:8]
         part_out[step, group] = partial[0:blocks * 8].reshape(blocks, 8, 128)
-        now["part"] = [
+        for n in range(1, blocks):
             send(
-                step, group, 6 + n, part_out.at[step, group, n], part_in.at[step, group, n],
+                step, group, 6, part_out.at[step, group, n], part_in.at[step, group, n],
                 device(codes[n]),
             )
-            for n in range(1, blocks)
-        ]
 
     def along_lanes(step, group):
         now = state[step, group]
@@ -269,19 +277,17 @@
     def give_back(step, group):
         now = state[step, group]
         owned = now["own"]
-        for n, copy in enumerate(now["part"], 1):
-            copy.wait_recv()
+        await_tiles(step, group, recv_sem, 6)
+        for n in range(1, blocks):
             owned = owned + part_in[step, group, n]
         coefficients = owned * energies
         now["own"] = coefficients
         coef_out[step, group] = coefficients
-        now["coef"] = [
+        for n in range(1, blocks):
             send(
-                step, group, 6 + blocks + n, coef_out.at[step, group],
+                step, group, 7, coef_out.at[step, group],
                 coef_in.at[step, group, opposite(codes[n])], device(codes[n]),
             )
-            for n in range(1, blocks)
-        ]
 
     def across_rows(step, group):
         now = state[step, group]
@@ -304,8 +310,8 @@
 
     def finish(step, group):
         now = state[step, group]
-        for copy in now["coef"]:
-            copy.wait_recv()
+        coefs = coef_in.at[step, group, pl.ds(1, blocks - 1)]
+        pltpu.make_async_copy(coefs, coefs, recv_sem.at[step, group, 7]).wait()
         around = jnp.concatenate(
             [now["own"]]
             + [coef_in[step, group, n] for n in range(1, blocks)]
@@ -345,7 +351,11 @@
         if step < DEGREE - 1:
             field[step, span] = result
         else:
-            out_ref[span] = result
+            acc[span] = result
+            stores.append(
+                pltpu.make_async_copy(acc.at[span], out_hbm.at[span], store_sem.at[group])
+            )
+            stores[-1].start()
 
     everyone = range(groups)
     for group in everyone:
@@ -363,6 +373,12 @@
 
     for copy in started:
         copy.wait_send()
+    for step in range(DEGREE):
+        for group in everyone:
+            await_tiles(step, group, send_sem, 6)
+            await_tiles(step, group, send_sem, 7)
+    for store in stores:
+        store.wait()
 
 
 def body(sizes, orbitals, potential, proj_values, point_cell, point_owner, point_slot, point_count, atom_energy):
@@ -373,17 +389,16 @@
     for size in sizes:
         blocks = blocks * min(3, size)
     seg_rows = (8 * blocks + 127) // 128 * 128
-    copies = 6 + 2 * blocks
+    copies = 8
     groups = GROUPS
     each_rows = norb // groups * rows
-    vmem = pl.BlockSpec(memory_space=pltpu.VMEM)
     smem = pl.BlockSpec(memory_space=pltpu.SMEM)
     hbm = pl.BlockSpec(memory_space=pltpu.HBM)
     return pl.pallas_call(
         functools.partial(kernel, sizes, groups),
         out_shape=jax.ShapeDtypeStruct(orbitals.shape, F32),
         in_specs=[hbm] * 6 + [smem, hbm],
-        out_specs=vmem,
+        out_specs=hbm,
         scratch_shapes=[
             pltpu.VMEM(orbitals.shape, F32),
             pltpu.VMEM(potential.shape, F32),
@@ -410,6 +425,7 @@
             pltpu.VMEM((points, seg_rows), BF16),
             pltpu.VMEM((nproj, points), F32),
             pltpu.SemaphoreType.DMA((7,)),
+            pltpu.SemaphoreType.DMA((groups,)),
             pltpu.SemaphoreType.DMA((DEGREE, groups, copies)),
             pltpu.SemaphoreType.DMA((DEGREE, groups, copies)),
         ],

time: 56.3 us -> 52.2 us (0.927)
  Pallas kernels: 53.5 us -> 49.5 us
    pallas_call x1, Pallas kernels: 53.5 us -> 49.5 us  [body(): pl.pallas_call(functools.partial(kernel, sizes, groups), out_shape=jax.Sh...]
where the time goes in v5:
time: 52.2 us; the launch traced here: 51.8 us
  Pallas kernels  49.5 us (95%)
  local copies, waits for them, and re-layouts  1.67 us (3%)
  between operations  0.66 us (1%)
    pallas_call x1, Pallas kernels, body(): pl.pallas_call(functools.partial(kernel, sizes, groups), out_shape=jax.Sh...  49.5 us
    unnamed x1, local copies, waits for them, and re-layouts  1.67 us

profile of v5, /device:TPU:0, one launch (start us, length us, event | category | flops | bytes accessed | tf_op | source)
XLA Modules:
  0.0 51.8 jit_solution(12497969746130747276)
XLA Ops:
  0.7 49.5 %shard_map.82 = f32[8,8,8,128]{3,2,1,0:T(8,128)} custom-call(f32[8,8,8,128]{3,2,1,0:T(8,128)} %orb_hbm.1, f32[8,8,128]{2,1,0:T(8,128)} %pot_hbm.1, f32[4,2048]{1,0:T(4,128)} %val_hbm.1, s32[1,2048]{1,0:T(1,128)} %bitcast.3, s32[1,2048]{1,0:T(1,128)} %bitcast.4, s32[1,2048]{1,0:T(1,128)} %bitcast.5, s32[1]{0:T(128)S(6)} %copy.10.count_ref, f32[4,160]{1,0:T(4,128)} %energy_hbm.1), custom_call_target="tpu_custom_call" | custom-call | tf_op jit(solution)/shard_map/pallas_call | solution.py:397
  50.1 1.7 %copy.11 = f32[8,8,8,128]{3,2,1,0:T(8,128)} copy(f32[8,8,8,128]{3,2,1,0:T(8,128)} %shard_map.82) | data formatting | bytes 524288

commit v6 on v5

--- a/solution.py
+++ b/solution.py
@@ -69,7 +69,7 @@
     out_hbm,
     orb_ref, pot_ref, val_ref, cell_ref, owner_ref, slot_ref, energy_ref,
     field, acc, x_low, x_high, y_in, z_out, z_in, part_out, part_in, coef_out, coef_in,
-    lane_hot, lane_turn, row_hot, seg_hot, seg_turn, masked, load_sem, store_sem, send_sem, recv_sem,
+    lane_hot, lane_turn, row_hot, seg_hot, seg_turn, masked, packed, around, load_sem, store_sem, send_sem, recv_sem,
 ):
     size_x, size_y, size_z = sizes
     norb, cx, cy, cz = orb_ref.shape
@@ -204,7 +204,7 @@
     for axis in range(3):
         remain = divided(coords[axis] - here[axis] + sizes[axis], sizes[axis])[1]
         block = block * spans[axis] + jnp.minimum(remain, 2)
-    segment = block * 8 + slot_ref[...]
+    segment = block * ATOM_DEV + slot_ref[...]
     at_seg = (lax.broadcasted_iota(jnp.int32, (seg_rows, points), 0) == segment).astype(F32)
     seg_hot[...] = at_seg.astype(BF16)
     seg_turn[...] = at_seg.T.astype(BF16)
@@ -224,6 +224,7 @@
         energies = jnp.where(lane_group == j, own, energies)
 
     used = nproj * each
+    around[...] = jnp.zeros(around.shape, F32)
 
     def begin(step, group):
         now = state[step, group]
@@ -255,7 +256,9 @@
             [partial[0:used] + partial[used:2 * used], jnp.zeros((128 - used, seg_rows), F32)], axis=0
         ).T
         now["own"] = partial[0:8]
-        part_out[step, group] = partial[0:blocks * 8].reshape(blocks, 8, 128)
+        packed[...] = partial
+        for n in range(1, blocks):
+            part_out[step, group, n] = packed[n * ATOM_DEV:n * ATOM_DEV + 8]
         for n in range(1, blocks):
             send(
                 step, group, 6, part_out.at[step, group, n], part_in.at[step, group, n],
@@ -312,13 +315,10 @@
         now = state[step, group]
         coefs = coef_in.at[step, group, pl.ds(1, blocks - 1)]
         pltpu.make_async_copy(coefs, coefs, recv_sem.at[step, group, 7]).wait()
-        around = jnp.concatenate(
-            [now["own"]]
-            + [coef_in[step, group, n] for n in range(1, blocks)]
-            + [jnp.zeros((seg_rows - 8 * blocks, 128), F32)],
-            axis=0,
-        )
-        high, low = split_two(around.T[0:used])
+        around[0:8] = now["own"]
+        for n in range(1, blocks):
+            around[n * ATOM_DEV:n * ATOM_DEV + 8] = coef_in[step, group, n]
+        high, low = split_two(around[...].T[0:used])
         spread = jnp.dot(
             jnp.concatenate([high, low], axis=0), seg_hot[...], preferred_element_type=F32
         )
@@ -388,7 +388,7 @@
     blocks = 1
     for size in sizes:
         blocks = blocks * min(3, size)
-    seg_rows = (8 * blocks + 127) // 128 * 128
+    seg_rows = (ATOM_DEV * blocks + 8 + 127) // 128 * 128
     copies = 8
     groups = GROUPS
     each_rows = norb // groups * rows
@@ -424,6 +424,8 @@
             pltpu.VMEM((seg_rows, points), BF16),
             pltpu.VMEM((points, seg_rows), BF16),
             pltpu.VMEM((nproj, points), F32),
+            pltpu.VMEM((seg_rows, 128), F32),
+            pltpu.VMEM((seg_rows, 128), F32),
             pltpu.SemaphoreType.DMA((7,)),
             pltpu.SemaphoreType.DMA((groups,)),
             pltpu.SemaphoreType.DMA((DEGREE, groups, copies)),

time: 52.2 us -> 52.1 us (level)
  no operation moved by 1% of the time
where the time goes in v6:
time: 52.1 us; the launch traced here: 51.7 us
  Pallas kernels  49.3 us (95%)
  local copies, waits for them, and re-layouts  1.67 us (3%)
  between operations  0.66 us (1%)
    pallas_call x1, Pallas kernels, body(): pl.pallas_call(functools.partial(kernel, sizes, groups), out_shape=jax.Sh...  49.3 us
    unnamed x1, local copies, waits for them, and re-layouts  1.67 us

profile of v6, /device:TPU:0, one launch (start us, length us, event | category | flops | bytes accessed | tf_op | source)
XLA Modules:
  0.0 51.7 jit_solution(107581991783364490)
XLA Ops:
  0.7 49.3 %shard_map.82 = f32[8,8,8,128]{3,2,1,0:T(8,128)} custom-call(f32[8,8,8,128]{3,2,1,0:T(8,128)} %orb_hbm.1, f32[8,8,128]{2,1,0:T(8,128)} %pot_hbm.1, f32[4,2048]{1,0:T(4,128)} %val_hbm.1, s32[1,2048]{1,0:T(1,128)} %bitcast.3, s32[1,2048]{1,0:T(1,128)} %bitcast.4, s32[1,2048]{1,0:T(1,128)} %bitcast.5, s32[1]{0:T(128)S(6)} %copy.10.count_ref, f32[4,160]{1,0:T(4,128)} %energy_hbm.1), custom_call_target="tpu_custom_call" | custom-call | tf_op jit(solution)/shard_map/pallas_call | solution.py:397
  50.0 1.7 %copy.11 = f32[8,8,8,128]{3,2,1,0:T(8,128)} copy(f32[8,8,8,128]{3,2,1,0:T(8,128)} %shard_map.82) | data formatting | bytes 524288
